TPU v7x, 256 devices: a whole 4x4x8 slice. The times are simulated.
256 devices in a mesh: dev: 128 (over x_lo, y, z, core), rep: 2 (over x_hi).
Axes of the slice: x: 4 (x_hi: 2, x_lo: 2; x = x_hi * 2 + x_lo), y: 4, z: 8, core: 2. Of those that a mesh axis runs over, the one named last changes fastest.
Arguments:
- pair_state: bfloat16 [512, 512, 128], P('dev', 'rep'), may hold values from -6 to 6
- token_pair_mask: int32 [512, 512], P('dev', 'rep'), may hold values 0 or 1
- alignment_state: bfloat16 [128, 512, 64], P('rep', 'dev'), may hold values from -6 to 6
- alignment_mask: int32 [128, 512], P('rep', 'dev'), may hold values 0 or 1
- input_weight: bfloat16 [128, 640], replicated, may hold values from -0.5 to 0.5
- output_weight: bfloat16 [128, 128], replicated, may hold values from -0.5 to 0.5
- alignment_weight: bfloat16 [64, 64], replicated, may hold values from -0.75 to 0.75
- outer_weight: bfloat16 [1024, 128], replicated, may hold values from -1 to 1
Outputs:
- pair_new: bfloat16 [512, 512, 128], P('dev', 'rep')
All inputs are finite; a program needn't handle non-finite values. No bound on the sum of `token_pair_mask` or of `alignment_mask` on one device may be relied on, other than what follows from the above.
Results may differ from a plain program's by a relative error of at most 0.011.
Values may be sent and summed in bfloat16 or wider, within the bound.
No kernel may reach another device: no remote copies, remote signals or barrier semaphores. Data moves between devices by JAX's collectives and lax.ppermute only.
A program may use at most 64 MiB of HBM per device.

v0:
```python
import jax
import jax.numpy as jnp
from jax import lax
from jax.sharding import Mesh, PartitionSpec as P

FACTOR_WIDTH = 32
ALIGNMENT_ROWS = 128
DEV = ("xl", "y", "z", "c")
PLANE = ("xl", "y", "c", "xh")
ALL = ("xl", "y", "z", "c", "xh")


def apply_layer_norm(values, axis):
    center = jnp.mean(values, axis=axis, keepdims=True)
    spread = jnp.mean((values - center) ** 2, axis=axis, keepdims=True)
    return (values - center) * lax.rsqrt(spread + 1e-05)


def factors(alignment_state, alignment_mask, alignment_weight):
    normed = apply_layer_norm(alignment_state.astype(jnp.float32), -1).astype(jnp.bfloat16)
    maskf = alignment_mask.astype(jnp.float32)
    fac_a = jnp.einsum(
        "szm,mc->zsc", normed, alignment_weight[:, :FACTOR_WIDTH], preferred_element_type=jnp.float32
    )
    fac_b = jnp.einsum(
        "szm,md->zds", normed, alignment_weight[:, FACTOR_WIDTH:], preferred_element_type=jnp.float32
    )
    fac_a = (fac_a * maskf.T[:, :, None]).astype(jnp.bfloat16)
    fac_b = (fac_b * maskf.T[:, None, :]).astype(jnp.bfloat16)
    return fac_a, fac_b


def shards(
    pair_state,
    token_pair_mask,
    alignment_state,
    alignment_mask,
    input_weight,
    output_weight,
    alignment_weight,
    outer_weight,
):
    rows, half, width = pair_state.shape
    points = rows * half
    seqs, _, _ = alignment_state.shape
    sizes = {name: lax.axis_size(name) for name in ALL}
    ny, nz, nc, nr = sizes["y"], sizes["z"], sizes["c"], sizes["xh"]
    devs = sizes["xl"] * ny * nz * nc
    depth = FACTOR_WIDTH * seqs

    fac_a, fac_b = factors(alignment_state, alignment_mask, alignment_weight)
    piece = fac_b.reshape(1, rows, depth)
    peers = sizes["xl"] * ny * nc * nr
    plane = lax.all_to_all(
        jnp.broadcast_to(piece, (peers, rows, depth)), PLANE, split_axis=0, concat_axis=0, tiled=True
    )
    plane = plane.reshape(sizes["xl"], ny, nc, nr, rows, depth)
    plane = lax.dynamic_index_in_dim(plane, lax.axis_index("xh"), 0, keepdims=False)
    plane = jnp.transpose(plane, (0, 1, 3, 2, 4)).reshape(ny * nc * rows, nr * depth)
    gathered = lax.all_gather(plane, "z", axis=0, tiled=True)
    other_a = lax.ppermute(fac_a, "xh", [(i, (i + 1) % nr) for i in range(nr)])
    first = lax.axis_index("xh") == 0
    both_a = jnp.stack([jnp.where(first, fac_a, other_a), jnp.where(first, other_a, fac_a)], 1)
    terms = jnp.einsum(
        "irsc,dcf->rdsif",
        both_a,
        outer_weight.reshape(FACTOR_WIDTH, FACTOR_WIDTH, width),
        preferred_element_type=jnp.float32,
    ) * (1.0 / ALIGNMENT_ROWS)
    terms = terms.astype(jnp.bfloat16).reshape(nr * depth, rows * width)

    state = pair_state.reshape(points, width).astype(jnp.float32)
    normed = apply_layer_norm(state, -1).astype(jnp.bfloat16)
    stacked = jnp.einsum(
        "pc,cf->fp", normed, input_weight[:, : 4 * width], preferred_element_type=jnp.float32
    ).reshape(2, 2, width, points)
    maskf = token_pair_mask.reshape(1, 1, points).astype(jnp.float32)
    pair_factors = (jax.nn.sigmoid(stacked[:, 0]) * stacked[:, 1] * maskf).astype(jnp.bfloat16)
    pair_factors = jnp.transpose(pair_factors.reshape(2, width, rows, half), (1, 0, 2, 3))
    pair_factors = pair_factors.reshape(width, 2 * rows, half)
    gate = jax.nn.sigmoid(
        jnp.dot(normed, input_weight[:, 4 * width :], preferred_element_type=jnp.float32)
    )
    swapped = lax.all_to_all(pair_factors, DEV, split_axis=0, concat_axis=0, tiled=True)
    swapped = swapped.reshape(devs, 2, rows, half)
    left = swapped[:, 0].reshape(devs * rows, half)
    right = swapped[:, 1].reshape(devs * rows, half)
    partial = lax.dot_general(
        left, right, (((1,), (1,)), ((), ())), preferred_element_type=jnp.float32
    ).astype(jnp.bfloat16)
    partial = jnp.transpose(partial.reshape(devs, rows, nr, half), (0, 2, 1, 3))
    back = lax.all_to_all(
        partial.reshape(devs * nr, rows, half), ALL, split_axis=0, concat_axis=0, tiled=True
    )
    back = back.reshape(devs, nr, points).astype(jnp.float32)
    tri_sum = (back[:, 0] + back[:, 1]).astype(jnp.bfloat16).astype(jnp.float32)
    tri_norm = apply_layer_norm(tri_sum, 0).astype(jnp.bfloat16)
    tri_out = gate * jnp.einsum(
        "cp,cd->pd", tri_norm, output_weight, preferred_element_type=jnp.float32
    )
    opm = jnp.dot(gathered, terms, preferred_element_type=jnp.float32)
    opm = opm.reshape(nz, ny, nc * rows, rows, width)
    opm = jnp.transpose(opm, (3, 1, 0, 2, 4)).reshape(points, width)
    return (state + opm + tri_out).astype(jnp.bfloat16).reshape(rows, half, width)


def solution(mesh):
    grid = Mesh(mesh.devices.reshape(2, 4, 8, 2, 2), ALL)
    inner = jax.shard_map(
        shards,
        mesh=grid,
        in_specs=(
            P(DEV, "xh", None),
            P(DEV, "xh"),
            P("xh", DEV, None),
            P("xh", DEV),
            P(),
            P(),
            P(),
            P(),
        ),
        out_specs=P(DEV, "xh", None),
        check_vma=False,
    )
    return inner
```

profile of v0, /device:TPU:1, one launch (start us, length us, event | category | flops | bytes accessed | tf_op | source)
XLA Modules:
  0.0 150.1 jit_solution(4870338255913895368)
XLA Ops:
  6.5 0.0 copy-start
  6.5 0.0 copy-start.1
  6.5 0.0 copy-start.7
  6.5 1.0 convert_reduce_fusion.1
  7.6 1.1 fusion.20
  8.7 1.0 fusion.21
  9.7 0.7 convert_bitcast_fusion
  10.4 1.0 fusion.8
  11.4 0.1 broadcast_in_dim.4
  11.5 1.0 broadcast_in_dim.5
  12.5 8.6 %all-to-all-start = ((bf16[32,4,2048]{2,1,0:T(4,128)(2,1)}), bf16[32,4,2048]{2,1,0:T(4,128)(2,1)S(1)}, u32[]{:S(2)}, u32[]{:S(2)}) async-start(bf16[32,4,2048]{2,1,0:T(4,128)(2,1)} %broadcast_in_dim.5), calls=%async_computation | async-start | bytes 1048576 | tf_op jit(solution)/shard_map/all_to_all | solution.py:54
  21.1 0.0 all-gather.2.cloned.1.call-start
  21.2 11.4 %all-to-all-done = bf16[32,4,2048]{2,1,0:T(4,128)(2,1)S(1)} async-done(((bf16[32,4,2048]{2,1,0:T(4,128)(2,1)}), bf16[32,4,2048]{2,1,0:T(4,128)(2,1)S(1)}, u32[]{:S(2)}, u32[]{:S(2)}) %all-to-all-start) | async-done | bytes 524320 | tf_op jit(solution)/shard_map/all_to_all | solution.py:54
  32.6 0.1 dynamic-slice_bitcast_fusion
  32.7 0.3 copy.54
  33.0 0.8 copy.84
  33.8 0.0 all-gather.2.cloned.1.call-update
  33.8 0.9 fusion.9
  34.7 0.7 collective-permute-start
  35.5 0.0 copy-done.1
  35.5 0.1 convert_reduce_fusion
  35.6 0.4 fusion.13
  36.0 0.0 copy-done.7
  36.1 3.2 %collective-permute-done = bf16[4,64,32]{1,2,0:T(8,128)(2,1)S(1)} collective-permute-done((bf16[4,64,32]{1,2,0:T(8,128)(2,1)S(1)}, bf16[4,64,32]{1,2,0:T(8,128)(2,1)S(1)}, u32[]{:S(2)}, u32[]{:S(2)}) %collective-permute-start) | collective-permute-done | bytes 16416 | tf_op jit(solution)/shard_map/ppermute | solution.py:61
  39.3 0.0 copy-done
  39.3 1.3 fusion
  40.6 8.3 %copy.58 = bf16[2,32,64,4,128]{4,3,2,1,0:T(4,128)(2,1)S(1)} copy(bf16[2,32,64,4,128]{4,2,1,0,3:T(8,128)(2,1)S(1)} %fusion) | data formatting | bytes 8388608 | tf_op jit(solution)/shard_map/convert_element_type | solution.py:70
  48.9 2.7 %copy.101 = bf16[512,8,4,128]{3,1,2,0:T(8,128)(2,1)} copy(bf16[512,8,4,128]{3,2,1,0:T(4,128)(2,1)S(1)} %bitcast.115) | data formatting | bytes 8388608
  51.6 6.4 %copy.74 = bf16[512,4096]{1,0:T(8,128)(2,1)} copy(bf16[512,4096]{0,1:T(8,128)(2,1)} %bitcast.116) | data formatting | bytes 8388608 | tf_op jit(solution)/shard_map/dot_general | solution.py:101
  58.0 12.4 %all-gather.2.cloned.1.call-done = bf16[256,4096]{1,0:T(8,128)(2,1)} async-done(((bf16[32,4096]{1,0:T(8,128)(2,1)}), bf16[256,4096]{1,0:T(8,128)(2,1)}) %all-gather.2.cloned.1.call-update) | async-done | bytes 2097168 | tf_op jit(solution)/shard_map/all_gather | solution.py:60
  70.4 0.0 copy-start.5
  70.4 4.1 %convolution_bitcast_fusion = f32[4,4,8,8,128]{4,3,0,1,2:T(8,128)S(1)} fusion(bf16[8,4,8,4096,1]{3,2,4,1,0:T(8,128)(2,1)} %bitcast.126, bf16[4,128,4096,1,1]{2,1,0,4,3:T(8,128)(2,1)} %bitcast.119), kind=kOutput, calls=%fused_computation.9 | convolution fusion | flops 1073741824 | bytes 6815744 | tf_op jit(solution)/shard_map/dot_general | solution.py:101
  74.6 1.1 fusion.15
  75.7 0.0 copy-start.3
  75.7 0.0 copy-done.5
  75.7 0.5 fusion.22
  76.2 0.2 copy-done.3
  76.4 0.2 fusion.35
  76.6 0.3 copy.78
  77.0 0.3 copy.79
  77.3 0.3 divide_multiply_fusion
  77.6 0.2 multiply_convert_fusion.1
  77.8 0.4 copy.64
  78.2 0.0 copy-start.4
  78.2 31.7 %all_to_all.15 = bf16[128,8,256]{2,1,0:T(8,128)(2,1)S(1)} all-to-all(bf16[128,8,256]{2,1,0:T(8,128)(2,1)S(1)} %copy.64), channel_id=1, replica_groups=mesh['xl'=2,'y'=4,'z'=8,'c'=2,'xh'=2] {'xl','y','z','c'}, dimensions={0} | all-to-all | bytes 1048576 | tf_op jit(solution)/shard_map/all_to_all | solution.py:84
  110.0 0.1 reshape.130
  110.1 0.2 slice_bitcast_fusion
  110.3 0.1 reshape_squeeze.6
  110.4 0.1 reshape_squeeze.7
  110.4 0.3 convolution_convert_fusion
  110.8 0.1 reshape.131
  110.9 0.0 copy-start.2
  110.9 0.0 copy-start.6
  110.9 1.0 copy.67
  111.9 8.2 %all-to-all-start.2 = ((bf16[256,4,256]{2,1,0:T(4,128)(2,1)}), bf16[256,4,256]{2,1,0:T(4,128)(2,1)S(1)}, u32[]{:S(2)}, u32[]{:S(2)}) async-start(bf16[256,4,256]{2,1,0:T(4,128)(2,1)} %bitcast.32), calls=%async_computation.2 | async-start | bytes 1048576 | tf_op jit(solution)/shard_map/all_to_all | solution.py:92
  120.2 0.0 copy-done.4
  120.2 1.1 fusion.3
  121.2 19.5 %all-to-all-done.2 = bf16[256,4,256]{2,1,0:T(4,128)(2,1)S(1)} async-done(((bf16[256,4,256]{2,1,0:T(4,128)(2,1)}), bf16[256,4,256]{2,1,0:T(4,128)(2,1)S(1)}, u32[]{:S(2)}, u32[]{:S(2)}) %all-to-all-start.2) | async-done | bytes 524320 | tf_op jit(solution)/shard_map/all_to_all | solution.py:92
  140.8 0.6 reshape.136
  141.4 0.8 fusion.33
  142.2 0.1 multiply_reduce_fusion
  142.3 0.0 copy-done.2
  142.3 0.0 copy-done.6
  142.3 1.0 fusion.5
  (11 shorter events, 0.1 us)
Async XLA Ops:
  6.5 32.8 %copy-start = (bf16[1024,128]{1,0:T(8,128)(2,1)S(1)}, bf16[1024,128]{1,0:T(8,128)(2,1)}, u32[]{:S(2)}) copy-start(bf16[1024,128]{1,0:T(8,128)(2,1)} %param.15) | copy-start | bytes 786436
  6.5 28.9 %copy-start.1 = (bf16[4,256,128]{2,1,0:T(8,128)(2,1)S(1)}, bf16[4,256,128]{2,1,0:T(8,128)(2,1)}, u32[]{:S(2)}) copy-start(bf16[4,256,128]{2,1,0:T(8,128)(2,1)} %param.8) | copy-start | bytes 786436
  6.5 29.5 %copy-start.7 = (s32[4,256]{1,0:T(4,128)S(1)}, s32[4,256]{1,0:T(4,128)}, u32[]{:S(2)}) copy-start(s32[4,256]{1,0:T(4,128)} %param.9) | copy-start | bytes 12292
  12.5 20.1 %all-to-all-start = ((bf16[32,4,2048]{2,1,0:T(4,128)(2,1)}), bf16[32,4,2048]{2,1,0:T(4,128)(2,1)S(1)}, u32[]{:S(2)}, u32[]{:S(2)}) async-start(bf16[32,4,2048]{2,1,0:T(4,128)(2,1)} %broadcast_in_dim.5), calls=%async_computation | async-start | bytes 1048576 | tf_op jit(solution)/shard_map/all_to_all | solution.py:54
  21.1 49.3 %all-gather.2.cloned.1.call-start = ((), (), s32[]{:S(2)}) async-start(), calls=%async_computation.3 | async-start | bytes 2359296 | tf_op jit(solution)/shard_map/all_gather | solution.py:60
  34.7 4.5 %collective-permute-start = (bf16[4,64,32]{1,2,0:T(8,128)(2,1)S(1)}, bf16[4,64,32]{1,2,0:T(8,128)(2,1)S(1)}, u32[]{:S(2)}, u32[]{:S(2)}) collective-permute-start(bf16[4,64,32]{1,2,0:T(8,128)(2,1)S(1)} %fusion.9), channel_id=1, source_target_pairs={{0,1},{1,0},{2,3},{3,2},{4,5},{5,4},{6,7},{7,6},{8,9},{9,8},{10,11... | collective-permute-start | bytes 49160 | tf_op jit(solution)/shard_map/ppermute | solution.py:61
  70.4 5.3 %copy-start.5 = (bf16[128,640]{1,0:T(8,128)(2,1)S(1)}, bf16[128,640]{1,0:T(8,128)(2,1)}, u32[]{:S(2)}) copy-start(bf16[128,640]{1,0:T(8,128)(2,1)} %param.12) | copy-start | bytes 491524
  75.7 0.7 copy-start.3
  78.2 41.9 %copy-start.4 = (bf16[1024,128]{1,0:T(8,128)(2,1)S(1)}, bf16[1024,128]{1,0:T(8,128)(2,1)}, u32[]{:S(2)}) copy-start(bf16[1024,128]{1,0:T(8,128)(2,1)} %copy-done.3) | copy-start | bytes 786436
  110.9 31.4 %copy-start.2 = (f32[1024,128]{1,0:T(8,128)S(1)}, f32[1024,128]{1,0:T(8,128)}, u32[]{:S(2)}) copy-start(f32[1024,128]{1,0:T(8,128)} %get-tuple-element.12) | copy-start | bytes 1572868
  110.9 31.4 %copy-start.6 = (bf16[128,128]{1,0:T(8,128)(2,1)S(1)}, bf16[128,128]{1,0:T(8,128)(2,1)}, u32[]{:S(2)}) copy-start(bf16[128,128]{1,0:T(8,128)(2,1)} %param.13) | copy-start | bytes 98308
  111.9 28.8 %all-to-all-start.2 = ((bf16[256,4,256]{2,1,0:T(4,128)(2,1)}), bf16[256,4,256]{2,1,0:T(4,128)(2,1)S(1)}, u32[]{:S(2)}, u32[]{:S(2)}) async-start(bf16[256,4,256]{2,1,0:T(4,128)(2,1)} %bitcast.32), calls=%async_computation.2 | async-start | bytes 1048576 | tf_op jit(solution)/shard_map/all_to_all | solution.py:92
Sparse Core Ops, SparseCore 0:
  34.0 36.4 all-gather.1
where the time goes:
time: 151 us; the launch traced here: 150 us
  waiting for transfers between devices  46.6 us (31%)
  blocking collectives  31.7 us (21%)
  local copies, waits for them, and re-layouts  23.5 us (16%)
  starting transfers between devices  17.6 us (12%)
  between operations  13.7 us (9%)
  matrix products  10.1 us (7%)
  other arithmetic  6.81 us (5%)
    all_to_all x1, blocking collectives, shards(): lax.all_to_all(pair_factors, DEV, split_axis=0, concat_axis=0, tiled=True)  31.7 us
    all_to_all x1, waiting for transfers between devices, shards(): lax.all_to_all(partial.reshape(devs * nr, rows, half), ALL, split_axis=0,...  19.5 us
    all_gather x1, waiting for transfers between devices, shards(): gathered = lax.all_gather(plane, 'z', axis=0, tiled=True)  12.4 us
    all_to_all x1, waiting for transfers between devices, shards(): lax.all_to_all(jnp.broadcast_to(piece, (peers, rows, depth)), PLANE, spli...  11.4 us
    all_to_all x1, starting transfers between devices, shards(): lax.all_to_all(jnp.broadcast_to(piece, (peers, rows, depth)), PLANE, spli...  8.59 us
    convert_element_type x1, local copies, waits for them, and re-layouts, shards(): terms = terms.astype(jnp.bfloat16).reshape(nr * depth, rows * width)  8.32 us
    all_to_all x1, starting transfers between devices, shards(): lax.all_to_all(partial.reshape(devs * nr, rows, half), ALL, split_axis=0,...  8.22 us
    dot_general x1, local copies, waits for them, and re-layouts, shards(): opm = jnp.dot(gathered, terms, preferred_element_type=jnp.float32)  6.42 us
  transfers between devices with their start and end apart: 4, of which 4 were waited for; matrix products, arithmetic and copies ran while one was open for 14% of the time, Pallas kernels for 0%

commit v1 on v0

v1 whole, which is shorter than its diff:
```python
import functools

import jax
import jax.numpy as jnp
from jax import lax
from jax.experimental import pallas as pl
from jax.experimental.pallas import tpu as pltpu
from jax.sharding import Mesh, PartitionSpec as P

FACTOR_WIDTH = 32
ALIGNMENT_ROWS = 128
VMEM_LIMIT = 56 * 1024 * 1024
PROJECT_LIMIT = 56 * 1024 * 1024
DEV = ("xl", "y", "z", "c")
PLANE = ("xl", "y", "c", "xh")
ALL = ("xl", "y", "z", "c", "xh")


def apply_layer_norm(values, axis):
    center = jnp.mean(values, axis=axis, keepdims=True)
    spread = jnp.mean((values - center) ** 2, axis=axis, keepdims=True)
    return (values - center) * lax.rsqrt(spread + 1e-05)


def normalize(values):
    values = values - jnp.mean(values, axis=-1, keepdims=True)
    spread = jnp.mean(values * values, axis=-1, keepdims=True)
    return values * lax.rsqrt(spread + 1e-05)


def factors_kernel(align_ref, align_mask_ref, align_weight_ref, first_ref, second_ref):
    seqs, tokens, _ = align_ref.shape
    align = jnp.swapaxes(align_ref[...].astype(jnp.float32), 0, 1)
    columns = [normalize(align[tok]) for tok in range(tokens)]
    both = lax.dot_general(
        align_weight_ref[...],
        jnp.concatenate(columns, 0).astype(jnp.bfloat16),
        (((0,), (1,)), ((), ())),
        preferred_element_type=jnp.float32,
    )
    align_mask = align_mask_ref[...].astype(jnp.float32)
    tiles = []
    for tok in range(tokens):
        part = both[:, tok * seqs : (tok + 1) * seqs] * align_mask[tok : tok + 1, :]
        first_ref[:, tok * seqs : (tok + 1) * seqs] = part[:FACTOR_WIDTH].astype(jnp.bfloat16)
        part = part[FACTOR_WIDTH:]
        tiles.append(jnp.concatenate([part[: FACTOR_WIDTH // 2], part[FACTOR_WIDTH // 2 :]], 1))
    second_ref[...] = jnp.swapaxes(jnp.stack(tiles), 0, 1).astype(jnp.bfloat16)


def factors(align, align_mask, align_weight):
    seqs, tokens, _ = align.shape
    return pl.pallas_call(
        factors_kernel,
        out_shape=(
            jax.ShapeDtypeStruct((FACTOR_WIDTH, tokens * seqs), jnp.bfloat16),
            jax.ShapeDtypeStruct((FACTOR_WIDTH // 2, tokens, 2 * seqs), jnp.bfloat16),
        ),
        compiler_params=pltpu.CompilerParams(vmem_limit_bytes=VMEM_LIMIT),
        name="factors",
    )(align, align_mask.T, align_weight)


def project_kernel(state_ref, mask_ref, weight_ref, out_ref):
    rows, half, width = state_ref.shape
    weight = weight_ref[:, : 4 * width]
    for row in range(rows):
        normed = normalize(state_ref[row].astype(jnp.float32)).astype(jnp.bfloat16)
        stacked = lax.dot_general(
            weight, normed, (((0,), (1,)), ((), ())), preferred_element_type=jnp.float32
        )
        maskf = mask_ref[row : row + 1, :].astype(jnp.float32)
        for side in range(2):
            opened = stacked[2 * side * width : (2 * side + 1) * width]
            linear = stacked[(2 * side + 1) * width : (2 * side + 2) * width]
            factor = jax.nn.sigmoid(opened) * linear * maskf
            out_ref[row, :, side * half : (side + 1) * half] = factor.astype(jnp.bfloat16)


def project(pair_state, mask, weight):
    rows, half, width = pair_state.shape
    return pl.pallas_call(
        project_kernel,
        out_shape=jax.ShapeDtypeStruct((rows, width, 2 * half), jnp.bfloat16),
        compiler_params=pltpu.CompilerParams(vmem_limit_bytes=PROJECT_LIMIT),
        name="project",
    )(pair_state, mask, weight)


def pack_kernel(grid, factor_ref, second_ref, send_ref):
    nx, ny, nz, nc = grid
    slices, tokens, lanes = second_ref.shape
    sides = factor_ref.shape[2]
    send_ref[:, :, :sides] = jnp.swapaxes(factor_ref[...].astype(jnp.float32), 0, 1).astype(jnp.bfloat16)
    pieces = second_ref[...].astype(jnp.float32).reshape(1, ny, 1, 2, nc, tokens, lanes)
    pieces = jnp.broadcast_to(pieces, (nx, ny, nz // 2, 2, nc, tokens, lanes))
    send_ref[:, :, sides:] = pieces.reshape(nx * ny * nz * nc, tokens, lanes).astype(jnp.bfloat16)


def pack(grid, factor, second):
    rows, width, sides = factor.shape
    return pl.pallas_call(
        functools.partial(pack_kernel, grid),
        out_shape=jax.ShapeDtypeStruct((width, rows, sides + second.shape[2]), jnp.bfloat16),
        compiler_params=pltpu.CompilerParams(vmem_limit_bytes=32 * 1024 * 1024),
        name="pack",
    )(factor, second)


def gate_kernel(state_ref, weight_ref, out_ref):
    values = state_ref[...].astype(jnp.float32)
    values = values - jnp.mean(values, axis=-1, keepdims=True)
    spread = jnp.mean(values * values, axis=-1, keepdims=True)
    normed = (values * lax.rsqrt(spread + 1e-05)).astype(jnp.bfloat16)
    out_ref[...] = jax.nn.sigmoid(
        jnp.dot(normed, weight_ref[:, 4 * state_ref.shape[1] :], preferred_element_type=jnp.float32)
    )


def gates(state, weight):
    return pl.pallas_call(
        gate_kernel,
        out_shape=jax.ShapeDtypeStruct(state.shape, jnp.float32),
        name="gates",
    )(state, weight)


def terms_kernel(place_ref, first_ref, weight_ref, out_ref):
    ny, nc, parts, rows = 4, 2, 2, 4
    columns = first_ref.shape[1] // parts
    width = weight_ref.shape[1]
    seqs = columns // rows
    own, came = first_ref[:, :columns], first_ref[:, columns:]
    mine = place_ref[2] == 0
    spread = jnp.concatenate([jnp.where(mine, own, came), jnp.where(mine, came, own)], 1)
    for core in range(nc):
        for turn in range(ny):
            for flip in range(2):
                piece = lax.rem(place_ref[0] + ny - turn, ny) * 2 + lax.rem(place_ref[3] + flip, 2)
                piece = piece * nc + lax.rem(place_ref[1] + core, nc)
                pair = [
                    weight_ref[pl.ds((dh * FACTOR_WIDTH // 2 + piece) * FACTOR_WIDTH, FACTOR_WIDTH), :]
                    for dh in range(2)
                ]
                product = lax.dot_general(
                    spread, jnp.concatenate(pair, 1), (((0,), (0,)), ((), ())), preferred_element_type=jnp.float32
                ).astype(jnp.bfloat16)
                for part in range(parts):
                    for row in range(rows):
                        start = part * columns + row * seqs
                        for dh in range(2):
                            at = ((((core * ny + turn) * 2 + flip) * parts + part) * 2 + dh) * seqs
                            out_ref[at : at + seqs, row * width : (row + 1) * width] = product[
                                start : start + seqs, dh * width : (dh + 1) * width
                            ]


def outer_terms(place, first, weight, rows):
    columns = first.shape[1]
    depth = FACTOR_WIDTH * columns // rows
    width = weight.shape[1]
    return pl.pallas_call(
        terms_kernel,
        in_specs=[
            pl.BlockSpec(memory_space=pltpu.SMEM),
            pl.BlockSpec(memory_space=pltpu.VMEM),
            pl.BlockSpec(memory_space=pltpu.VMEM),
        ],
        out_shape=jax.ShapeDtypeStruct((depth, rows * width), jnp.bfloat16),
        cost_estimate=pl.CostEstimate(
            flops=2 * depth * rows * width * FACTOR_WIDTH, bytes_accessed=2 * depth * rows * width, transcendentals=0
        ),
        compiler_params=pltpu.CompilerParams(vmem_limit_bytes=32 * 1024 * 1024),
        name="outer_terms",
    )(place, first, weight)


def compact(values):
    groups, rows, lanes = values.shape
    pairs = values.reshape(groups // 2, 2, rows, lanes)
    return jnp.concatenate([pairs[:, 0], pairs[:, 1]], 1).reshape(groups * rows, lanes)


def partial_kernel(swapped_ref, out_ref, table_ref):
    devs, rows, lanes = swapped_ref.shape
    parts = 2
    half = out_ref.shape[2]
    values = compact(swapped_ref[...].astype(jnp.float32))
    left = values[:, :half].astype(jnp.bfloat16)
    right = values[:, half : 2 * half].astype(jnp.bfloat16)
    for part in range(parts):
        product = lax.dot_general(
            left,
            right[part * half : (part + 1) * half],
            (((1,), (1,)), ((), ())),
            preferred_element_type=jnp.float32,
        )
        product = product.reshape(devs // 2, 2 * rows, half)
        product = jnp.stack([product[:, :rows], product[:, rows:]], 1).reshape(devs, rows, half)
        out_ref[part * devs : (part + 1) * devs] = product.astype(jnp.bfloat16)
    table = [values[part * half : (part + 1) * half, 2 * half :] for part in range(parts)]
    table_ref[...] = jnp.concatenate(table, 1).astype(jnp.bfloat16)


def partials(swapped, half):
    devs, rows, lanes = swapped.shape
    return pl.pallas_call(
        partial_kernel,
        out_shape=(
            jax.ShapeDtypeStruct((2 * devs, rows, half), jnp.bfloat16),
            jax.ShapeDtypeStruct((half, 2 * (lanes - 2 * half)), jnp.bfloat16),
        ),
        compiler_params=pltpu.CompilerParams(vmem_limit_bytes=32 * 1024 * 1024),
        name="partials",
    )(swapped)


def shards(
    pair_state,
    token_pair_mask,
    alignment_state,
    alignment_mask,
    input_weight,
    output_weight,
    alignment_weight,
    outer_weight,
):
    rows, half, width = pair_state.shape
    points = rows * half
    sizes = [lax.axis_size(name) for name in ALL]
    nx, ny, nz, nc, nr = sizes
    seqs = alignment_state.shape[0]
    devs = nx * ny * nz * nc
    place = jnp.stack([lax.axis_index(name) for name in ("y", "c", "xh", "z")])
    place = place.astype(jnp.int32) % jnp.array([ny, nc, nr, 2], jnp.int32)

    fac_a, fac_b = factors(alignment_state, alignment_mask, alignment_weight)
    fac_b = lax.ppermute(fac_b, ("xl", "xh"), [(0, 0), (1, 2), (2, 1), (3, 3)])
    swap = [(0, 1), (1, 0)]
    came_a = lax.ppermute(fac_a, "xh", swap)
    send = pack((nx, ny, nz, nc), project(pair_state, token_pair_mask, input_weight), fac_b)
    swapped = lax.all_to_all(send, DEV, split_axis=0, concat_axis=0, tiled=True)
    terms = outer_terms(place, jnp.concatenate([fac_a, came_a], 1), outer_weight, rows)
    state = pair_state.reshape(points, width)
    gate = gates(state, input_weight)
    swapped, terms, gate = lax.optimization_barrier((swapped, terms, gate))
    partial, table = partials(swapped, half)
    back = lax.all_to_all(partial, ("xh",) + DEV, split_axis=0, concat_axis=0, tiled=True)

    flipped = lax.ppermute(table, "z", [(i, i ^ 1) for i in range(nz)])
    turns = [jnp.concatenate([table, flipped], 1)]
    for turn in range(1, ny):
        turns.append(lax.ppermute(turns[0], "y", [(i, (i + turn) % ny) for i in range(ny)]))
    turns += [lax.ppermute(value, "c", swap) for value in turns]
    opm = jnp.zeros((half, rows * width), jnp.float32)
    depth = turns[0].shape[1]
    for index, value in enumerate(turns):
        opm = opm + jnp.dot(
            value, terms[index * depth : (index + 1) * depth], preferred_element_type=jnp.float32
        )

    back = back.reshape(nr, devs, points).astype(jnp.float32)
    tri_sum = (back[0] + back[1]).astype(jnp.bfloat16).astype(jnp.float32)
    tri_norm = apply_layer_norm(tri_sum, 0).astype(jnp.bfloat16)
    tri_out = gate * jnp.einsum(
        "cp,cd->pd", tri_norm, output_weight, preferred_element_type=jnp.float32
    )
    opm = (opm * (1.0 / ALIGNMENT_ROWS)).reshape(half, rows, width)
    opm = jnp.transpose(opm, (1, 0, 2)).reshape(points, width)
    return (state.astype(jnp.float32) + opm + tri_out).astype(jnp.bfloat16).reshape(rows, half, width)


def solution(mesh):
    grid = Mesh(mesh.devices.reshape(2, 4, 8, 2, 2), ALL)
    inner = jax.shard_map(
        shards,
        mesh=grid,
        in_specs=(
            P(DEV, "xh", None),
            P(DEV, "xh"),
            P("xh", DEV, None),
            P("xh", DEV),
            P(),
            P(),
            P(),
            P(),
        ),
        out_specs=P(DEV, "xh", None),
        check_vma=False,
    )
    return inner
```

time: 151 us -> 86.9 us (0.58)
  blocking collectives: 31.7 us -> 0 us
  waiting for transfers between devices: 46.6 us -> 23.4 us
  starting transfers between devices: 17.6 us -> 39.6 us
  local copies, waits for them, and re-layouts: 23.5 us -> 3.17 us
  between operations: 13.7 us -> 0.24 us
  Pallas kernels: 0 us -> 11 us
  other arithmetic: 6.81 us -> 2.17 us
  matrix products: 10.1 us -> 6.81 us
    all_to_all x1 -> x0, blocking collectives: 31.7 us -> none  [shards(): lax.all_to_all(pair_factors, DEV, split_axis=0, concat_axis=0, tiled=True)]
    ppermute x1 -> x10, starting transfers between devices: 0.71 us -> 16.2 us  [the longest x4 6.41 us: shards(): turns += [lax.ppermute(value, 'c', swap) for value in turns]]
    all_to_all x2, waiting for transfers between devices: 31 us -> 16 us  [the longest x1 12.4 us: shards(): swapped = lax.all_to_all(send, DEV, split_axis=0, concat_axis=0, tiled=True)]
    all_gather x1 -> x0, waiting for transfers between devices: 12.4 us -> none  [shards(): gathered = lax.all_gather(plane, 'z', axis=0, tiled=True)]
    pallas_call x0 -> x6, Pallas kernels: none -> 11 us  [the longest x1 2.58 us: project(): pl.pallas_call(project_kernel, out_shape=jax.ShapeDtypeStruct((rows, widt...]
    convert_element_type x2 -> x0, local copies, waits for them, and re-layouts: 8.96 us -> none  [the longest x1 8.32 us: shards(): terms = terms.astype(jnp.bfloat16).reshape(nr * depth, rows * width)]
    all_to_all x2, starting transfers between devices: 16.8 us -> 23.4 us  [the longest x1 16.9 us: shards(): swapped = lax.all_to_all(send, DEV, split_axis=0, concat_axis=0, tiled=True)]
    dot_general x1 -> x0, local copies, waits for them, and re-layouts: 6.42 us -> none  [shards(): opm = jnp.dot(gathered, terms, preferred_element_type=jnp.float32)]
  transfers between devices with their start and end apart: 4 -> 12, of which waited for: 4 -> 7; matrix products, arithmetic and copies ran while one was open for 14% -> 9% of each run, Pallas kernels for 0% -> 8%
where the time goes in v1:
time: 86.9 us; the launch traced here: 86.3 us
  starting transfers between devices  39.6 us (46%)
  waiting for transfers between devices  23.4 us (27%)
  Pallas kernels  11 us (13%)
  matrix products  6.81 us (8%)
  local copies, waits for them, and re-layouts  3.17 us (4%)
  other arithmetic  2.17 us (2%)
    all_to_all x1, starting transfers between devices, shards(): swapped = lax.all_to_all(send, DEV, split_axis=0, concat_axis=0, tiled=True)  16.9 us
    all_to_all x1, waiting for transfers between devices, shards(): swapped = lax.all_to_all(send, DEV, split_axis=0, concat_axis=0, tiled=True)  12.4 us
    dot_general x8, matrix products, shards(): jnp.dot(value, terms[index * depth:(index + 1) * depth], preferred_elemen...  6.54 us
    all_to_all x1, starting transfers between devices, shards(): lax.all_to_all(partial, ('xh',) + DEV, split_axis=0, concat_axis=0, tiled...  6.54 us
    ppermute x4, starting transfers between devices, shards(): turns += [lax.ppermute(value, 'c', swap) for value in turns]  6.41 us
    ppermute x3, starting transfers between devices, shards(): lax.ppermute(turns[0], 'y', [(i, (i + turn) % ny) for i in range(ny)])  5.95 us
    ppermute x1, waiting for transfers between devices, shards(): flipped = lax.ppermute(table, 'z', [(i, i ^ 1) for i in range(nz)])  4.01 us
    all_to_all x1, waiting for transfers between devices, shards(): lax.all_to_all(partial, ('xh',) + DEV, split_axis=0, concat_axis=0, tiled...  3.59 us
  transfers between devices with their start and end apart: 12, of which 7 were waited for; matrix products, arithmetic and copies ran while one was open for 9% of the time, Pallas kernels for 8%

profile of v1, /device:TPU:1, one launch (start us, length us, event | category | flops | bytes accessed | tf_op | source)
XLA Modules:
  0.0 86.3 jit_solution(11990858049336926711)
XLA Ops:
  0.0 0.0 copy-start
  0.0 0.0 copy-start.4
  0.0 1.9 %factors.1 = (bf16[32,256]{1,0:T(8,128)(2,1)}, bf16[16,4,128]{2,1,0:T(4,128)(2,1)}) custom-call(bf16[64,4,64]{2,1,0:T(4,128)(2,1)} %align_ref.1, s32[4,64]{1,0:T(4,128)} %bitcast.42, bf16[64,64]{1,0:T(8,128)(2,1)} %align_weight_ref.1), custom_call_target="tpu_custom_call" | custom-call | tf_op jit(solution)/shard_map/factors/pallas_call | solution.py:53
  1.9 0.0 copy-start.7
  1.9 1.5 %collective-permute-start = (bf16[16,4,128]{2,1,0:T(4,128)(2,1)}, bf16[16,4,128]{2,1,0:T(4,128)(2,1)S(1)}, u32[]{:S(2)}, u32[]{:S(2)}) collective-permute-start(bf16[16,4,128]{2,1,0:T(4,128)(2,1)} %get-tuple-element.12), channel_id=1, source_target_pairs={{0,0},{1,128},{128,1},{129,129},{2,2},{3,130},{130,3},{131,131},{4... | collective-permute-start | bytes 49160 | tf_op jit(solution)/shard_map/ppermute | solution.py:238
  3.4 2.6 %project.1.factor_ref = bf16[4,128,512]{2,1,0:T(8,128)(2,1)} custom-call(bf16[4,256,128]{2,1,0:T(8,128)(2,1)} %state_ref.1, s32[4,256]{1,0:T(4,128)} %mask_ref.1, bf16[128,640]{1,0:T(8,128)(2,1)} %weight_ref.5), custom_call_target="tpu_custom_call" | custom-call | tf_op jit(solution)/shard_map/project/pallas_call | solution.py:82
  6.0 0.0 collective-permute-done.second_ref
  6.0 0.0 copy-start.3
  6.0 1.0 %copy-done.3 = bf16[4,128,512]{2,1,0:T(8,128)(2,1)S(1)} copy-done((bf16[4,128,512]{2,1,0:T(8,128)(2,1)S(1)}, bf16[4,128,512]{2,1,0:T(8,128)(2,1)}, u32[]{:S(2)}) %copy-start.3) | copy-done | bytes 524312
  7.1 1.2 %pack.1 = bf16[128,4,640]{2,1,0:T(4,128)(2,1)} custom-call(bf16[4,128,512]{2,1,0:T(8,128)(2,1)S(1)} %copy-done.3, bf16[16,4,128]{2,1,0:T(4,128)(2,1)S(1)} %collective-permute-done.second_ref), custom_call_target="tpu_custom_call" | custom-call | tf_op jit(solution)/shard_map/pack/pallas_call | solution.py:102
  8.2 16.9 %all-to-all-start = ((bf16[128,4,640]{2,1,0:T(4,128)(2,1)}), bf16[128,4,640]{2,1,0:T(4,128)(2,1)S(1)}, u32[]{:S(2)}, u32[]{:S(2)}) async-start(bf16[128,4,640]{2,1,0:T(4,128)(2,1)} %pack.1), calls=%async_computation | async-start | bytes 1310720 | tf_op jit(solution)/shard_map/all_to_all | solution.py:242
  25.1 1.8 %collective-permute-start.1 = (bf16[32,256]{1,0:T(8,128)(2,1)}, bf16[32,256]{1,0:T(8,128)(2,1)S(1)}, u32[]{:S(2)}, u32[]{:S(2)}) collective-permute-start(bf16[32,256]{1,0:T(8,128)(2,1)} %get-tuple-element.13), channel_id=1, source_target_pairs={{0,1},{1,0},{2,3},{3,2},{4,5},{5,4},{6,7},{7,6},{8,9},{9,8},{10,11... | collective-permute-start | bytes 49160 | tf_op jit(solution)/shard_map/ppermute | solution.py:240
  26.9 0.9 and_select_fusion.place_ref
  27.8 2.3 %gates.1 = f32[1024,128]{1,0:T(8,128)} custom-call(bf16[1024,128]{1,0:T(8,128)(2,1)} %bitcast.37, bf16[128,640]{1,0:T(8,128)(2,1)} %weight_ref.5), custom_call_target="tpu_custom_call" | custom-call | tf_op jit(solution)/shard_map/gates/pallas_call | solution.py:121
  30.0 0.1 collective-permute-done.1
  30.1 0.0 copy-done.7
  30.1 0.0 copy-done.4
  30.1 1.8 %outer_terms.1 = bf16[4096,512]{1,0:T(8,128)(2,1)S(1)} custom-call(s32[4]{0:T(128)S(1)} %and_select_fusion.place_ref, bf16[32,512]{1,0:T(8,128)(2,1)S(1)} %pad_maximum_fusion.first_ref, bf16[1024,128]{1,0:T(8,128)(2,1)S(1)} %copy-done.4), custom_call_target="tpu_custom_call" | custom-call | flops 134217728 | bytes 4194304 | tf_op jit(solution)/shard_map/outer_terms/pallas_call | solution.py:162
  31.9 0.0 copy-start.1
  32.0 1.9 %copy-done.1 = bf16[4096,512]{1,0:T(8,128)(2,1)} copy-done((bf16[4096,512]{1,0:T(8,128)(2,1)}, bf16[4096,512]{1,0:T(8,128)(2,1)S(1)}, u32[]{:S(2)}) %copy-start.1) | copy-done | bytes 4194328
  33.9 12.4 %all-to-all-done.swapped_ref = bf16[128,4,640]{2,1,0:T(4,128)(2,1)S(1)} async-done(((bf16[128,4,640]{2,1,0:T(4,128)(2,1)}), bf16[128,4,640]{2,1,0:T(4,128)(2,1)S(1)}, u32[]{:S(2)}, u32[]{:S(2)}) %all-to-all-start) | async-done | bytes 655392 | tf_op jit(solution)/shard_map/all_to_all | solution.py:242
  46.3 1.2 %partials.1 = (bf16[256,4,256]{2,1,0:T(4,128)(2,1)}, bf16[256,256]{1,0:T(8,128)(2,1)S(1)}) custom-call(bf16[128,4,640]{2,1,0:T(4,128)(2,1)S(1)} %all-to-all-done.swapped_ref), custom_call_target="tpu_custom_call" | custom-call | tf_op jit(solution)/shard_map/partials/pallas_call | solution.py:207
  47.5 0.6 collective-permute-start.2
  48.1 4.0 %collective-permute-done.2 = bf16[256,256]{1,0:T(8,128)(2,1)S(1)} collective-permute-done((bf16[256,256]{1,0:T(8,128)(2,1)S(1)}, bf16[256,256]{1,0:T(8,128)(2,1)S(1)}, u32[]{:S(2)}, u32[]{:S(2)}) %collective-permute-start.2) | collective-permute-done | bytes 131104 | tf_op jit(solution)/shard_map/ppermute | solution.py:250
  52.2 3.4 %collective-permute-start.4 = (bf16[256,512]{1,0:T(8,128)(2,1)S(1)}, bf16[256,512]{1,0:T(8,128)(2,1)S(1)}, u32[]{:S(2)}, u32[]{:S(2)}) collective-permute-start(bf16[256,512]{1,0:T(8,128)(2,1)S(1)} %constant_dynamic-update-slice_fusion), channel_id=1, source_target_pairs={{0,64},{32,96},{64,0},{96,32},{1,65},{33,97},{65,1},{97,33},{2,66}... | collective-permute-start | bytes 786440 | tf_op jit(solution)/shard_map/ppermute | solution.py:253
  55.6 1.1 %collective-permute-start.5 = (bf16[256,512]{1,0:T(8,128)(2,1)S(1)}, bf16[256,512]{1,0:T(8,128)(2,1)S(1)}, u32[]{:S(2)}, u32[]{:S(2)}) collective-permute-start(bf16[256,512]{1,0:T(8,128)(2,1)S(1)} %constant_dynamic-update-slice_fusion), channel_id=1, source_target_pairs={{0,96},{32,0},{64,32},{96,64},{1,97},{33,1},{65,33},{97,65},{2,98}... | collective-permute-start | bytes 786440 | tf_op jit(solution)/shard_map/ppermute | solution.py:253
  56.6 6.5 %all-to-all-start.1 = ((bf16[256,4,256]{2,1,0:T(4,128)(2,1)}), bf16[256,4,256]{2,1,0:T(4,128)(2,1)S(1)}, u32[]{:S(2)}, u32[]{:S(2)}) async-start(bf16[256,4,256]{2,1,0:T(4,128)(2,1)} %get-tuple-element.18), calls=%async_computation.1 | async-start | bytes 1048576 | tf_op jit(solution)/shard_map/all_to_all | solution.py:248
  63.2 0.0 copy-start.2
  63.2 1.5 %collective-permute-start.3 = (bf16[256,512]{1,0:T(8,128)(2,1)S(1)}, bf16[256,512]{1,0:T(8,128)(2,1)S(1)}, u32[]{:S(2)}, u32[]{:S(2)}) collective-permute-start(bf16[256,512]{1,0:T(8,128)(2,1)S(1)} %constant_dynamic-update-slice_fusion), channel_id=1, source_target_pairs={{0,32},{32,64},{64,96},{96,0},{1,33},{33,65},{65,97},{97,1},{2,34}... | collective-permute-start | bytes 786440 | tf_op jit(solution)/shard_map/ppermute | solution.py:253
  64.7 0.9 collective-permute-start.6
  65.5 0.0 collective-permute-done.4
  65.5 0.1 collective-permute-start.8
  65.6 1.3 %fusion.19 = f32[256,512]{1,0:T(8,128)S(1)} fusion(bf16[256,512]{1,0:T(8,128)(2,1)S(1)} %collective-permute-done.4, bf16[4096,512]{1,0:T(8,128)(2,1)} %copy-done.1), kind=kOutput, calls=%fused_computation.26 | convolution fusion | flops 134217728 | bytes 1310720 | tf_op jit(solution)/shard_map/dot_general | solution.py:258
  67.0 0.1 collective-permute-done.5
  67.1 1.3 %fusion.17 = f32[256,512]{1,0:T(8,128)S(1)} fusion(bf16[256,512]{1,0:T(8,128)(2,1)S(1)} %collective-permute-done.5, bf16[4096,512]{1,0:T(8,128)(2,1)} %copy-done.1), kind=kOutput, calls=%fused_computation.24 | convolution fusion | flops 134217728 | bytes 1310720 | tf_op jit(solution)/shard_map/dot_general | solution.py:258
  68.4 2.1 %collective-permute-start.9 = (bf16[256,512]{1,0:T(8,128)(2,1)S(1)}, bf16[256,512]{1,0:T(8,128)(2,1)S(1)}, u32[]{:S(2)}, u32[]{:S(2)}) collective-permute-start(bf16[256,512]{1,0:T(8,128)(2,1)S(1)} %collective-permute-done.5), channel_id=1, source_target_pairs={{0,2},{2,0},{1,3},{3,1},{4,6},{6,4},{5,7},{7,5},{8,10},{10,8},{9,1... | collective-permute-start | bytes 786440 | tf_op jit(solution)/shard_map/ppermute | solution.py:254
  70.5 2.6 %collective-permute-done.3 = bf16[256,512]{1,0:T(8,128)(2,1)S(1)} collective-permute-done((bf16[256,512]{1,0:T(8,128)(2,1)S(1)}, bf16[256,512]{1,0:T(8,128)(2,1)S(1)}, u32[]{:S(2)}, u32[]{:S(2)}) %collective-permute-start.3) | collective-permute-done | bytes 262176 | tf_op jit(solution)/shard_map/ppermute | solution.py:253
  73.1 1.3 %fusion.21 = f32[256,512]{1,0:T(8,128)S(1)} fusion(bf16[256,512]{1,0:T(8,128)(2,1)S(1)} %collective-permute-done.3, bf16[4096,512]{1,0:T(8,128)(2,1)} %copy-done.1), kind=kOutput, calls=%fused_computation.28 | convolution fusion | flops 134217728 | bytes 1310720 | tf_op jit(solution)/shard_map/dot_general | solution.py:258
  74.5 0.0 collective-permute-done.6
  74.5 1.3 %fusion.15 = f32[256,512]{1,0:T(8,128)S(1)} fusion(bf16[256,512]{1,0:T(8,128)(2,1)S(1)} %collective-permute-done.6, bf16[4096,512]{1,0:T(8,128)(2,1)} %copy-done.1), kind=kOutput, calls=%fused_computation.22 | convolution fusion | flops 134217728 | bytes 1310720 | tf_op jit(solution)/shard_map/dot_general | solution.py:258
  75.8 0.0 copy-done.2
  75.8 0.3 fusion.6
  76.1 3.3 %collective-permute-start.7 = (bf16[256,512]{1,0:T(8,128)(2,1)S(1)}, bf16[256,512]{1,0:T(8,128)(2,1)S(1)}, u32[]{:S(2)}, u32[]{:S(2)}) collective-permute-start(bf16[256,512]{1,0:T(8,128)(2,1)S(1)} %collective-permute-done.3), channel_id=1, source_target_pairs={{0,2},{2,0},{1,3},{3,1},{4,6},{6,4},{5,7},{7,5},{8,10},{10,8},{9,1... | collective-permute-start | bytes 786440 | tf_op jit(solution)/shard_map/ppermute | solution.py:254
  79.5 0.0 collective-permute-done.8
  79.5 0.3 fusion.12
  79.8 0.0 collective-permute-done.9
  79.8 0.3 fusion.10
  80.1 0.0 copy-start.5
  80.1 0.0 copy-start.6
  80.1 0.5 collective-permute-done.7
  80.7 0.3 fusion.3
  81.0 3.6 %all-to-all-done.1 = bf16[256,4,256]{2,1,0:T(4,128)(2,1)S(1)} async-done(((bf16[256,4,256]{2,1,0:T(4,128)(2,1)}), bf16[256,4,256]{2,1,0:T(4,128)(2,1)S(1)}, u32[]{:S(2)}, u32[]{:S(2)}) %all-to-all-start.1) | async-done | bytes 524320 | tf_op jit(solution)/shard_map/all_to_all | solution.py:248
  84.6 0.1 convert_element_type.26
  84.7 0.3 fusion.28
  85.0 0.1 copy.12
  85.2 0.1 multiply_reduce_fusion
  85.2 0.0 copy-done
  85.2 0.3 fusion.24
  85.5 0.0 copy-done.5
  85.5 0.0 copy-done.6
  85.5 0.8 fusion.9
  (7 shorter events, 0.1 us)
Async XLA Ops:
  0.0 85.2 %copy-start = (bf16[128,128]{1,0:T(8,128)(2,1)S(1)}, bf16[128,128]{1,0:T(8,128)(2,1)}, u32[]{:S(2)}) copy-start(bf16[128,128]{1,0:T(8,128)(2,1)} %param.14) | copy-start | bytes 98308
  0.0 30.1 %copy-start.4 = (bf16[1024,128]{1,0:T(8,128)(2,1)S(1)}, bf16[1024,128]{1,0:T(8,128)(2,1)}, u32[]{:S(2)}) copy-start(bf16[1024,128]{1,0:T(8,128)(2,1)} %weight_ref.4) | copy-start | bytes 786436
  1.9 28.2 %copy-start.7 = (bf16[32,256]{1,0:T(8,128)(2,1)S(1)}, bf16[32,256]{1,0:T(8,128)(2,1)}, u32[]{:S(2)}) copy-start(bf16[32,256]{1,0:T(8,128)(2,1)} %get-tuple-element.13) | copy-start | bytes 49156
  1.9 4.1 %collective-permute-start = (bf16[16,4,128]{2,1,0:T(4,128)(2,1)}, bf16[16,4,128]{2,1,0:T(4,128)(2,1)S(1)}, u32[]{:S(2)}, u32[]{:S(2)}) collective-permute-start(bf16[16,4,128]{2,1,0:T(4,128)(2,1)} %get-tuple-element.12), channel_id=1, source_target_pairs={{0,0},{1,128},{128,1},{129,129},{2,2},{3,130},{130,3},{131,131},{4... | collective-permute-start | bytes 49160 | tf_op jit(solution)/shard_map/ppermute | solution.py:238
  6.0 1.0 %copy-start.3 = (bf16[4,128,512]{2,1,0:T(8,128)(2,1)S(1)}, bf16[4,128,512]{2,1,0:T(8,128)(2,1)}, u32[]{:S(2)}) copy-start(bf16[4,128,512]{2,1,0:T(8,128)(2,1)} %project.1.factor_ref) | copy-start | bytes 1572868
  8.2 38.1 %all-to-all-start = ((bf16[128,4,640]{2,1,0:T(4,128)(2,1)}), bf16[128,4,640]{2,1,0:T(4,128)(2,1)S(1)}, u32[]{:S(2)}, u32[]{:S(2)}) async-start(bf16[128,4,640]{2,1,0:T(4,128)(2,1)} %pack.1), calls=%async_computation | async-start | bytes 1310720 | tf_op jit(solution)/shard_map/all_to_all | solution.py:242
  25.1 5.0 %collective-permute-start.1 = (bf16[32,256]{1,0:T(8,128)(2,1)}, bf16[32,256]{1,0:T(8,128)(2,1)S(1)}, u32[]{:S(2)}, u32[]{:S(2)}) collective-permute-start(bf16[32,256]{1,0:T(8,128)(2,1)} %get-tuple-element.13), channel_id=1, source_target_pairs={{0,1},{1,0},{2,3},{3,2},{4,5},{5,4},{6,7},{7,6},{8,9},{9,8},{10,11... | collective-permute-start | bytes 49160 | tf_op jit(solution)/shard_map/ppermute | solution.py:240
  31.9 2.0 %copy-start.1 = (bf16[4096,512]{1,0:T(8,128)(2,1)}, bf16[4096,512]{1,0:T(8,128)(2,1)S(1)}, u32[]{:S(2)}) copy-start(bf16[4096,512]{1,0:T(8,128)(2,1)S(1)} %outer_terms.1) | copy-start | bytes 12582916
  47.5 4.6 %collective-permute-start.2 = (bf16[256,256]{1,0:T(8,128)(2,1)S(1)}, bf16[256,256]{1,0:T(8,128)(2,1)S(1)}, u32[]{:S(2)}, u32[]{:S(2)}) collective-permute-start(bf16[256,256]{1,0:T(8,128)(2,1)S(1)} %get-tuple-element.15), channel_id=1, source_target_pairs={{0,4},{4,0},{8,12},{12,8},{16,20},{20,16},{24,28},{28,24},{1,5},{5... | collective-permute-start | bytes 393224 | tf_op jit(solution)/shard_map/ppermute | solution.py:250
  52.2 13.4 %collective-permute-start.4 = (bf16[256,512]{1,0:T(8,128)(2,1)S(1)}, bf16[256,512]{1,0:T(8,128)(2,1)S(1)}, u32[]{:S(2)}, u32[]{:S(2)}) collective-permute-start(bf16[256,512]{1,0:T(8,128)(2,1)S(1)} %constant_dynamic-update-slice_fusion), channel_id=1, source_target_pairs={{0,64},{32,96},{64,0},{96,32},{1,65},{33,97},{65,1},{97,33},{2,66}... | collective-permute-start | bytes 786440 | tf_op jit(solution)/shard_map/ppermute | solution.py:253
  55.6 11.5 %collective-permute-start.5 = (bf16[256,512]{1,0:T(8,128)(2,1)S(1)}, bf16[256,512]{1,0:T(8,128)(2,1)S(1)}, u32[]{:S(2)}, u32[]{:S(2)}) collective-permute-start(bf16[256,512]{1,0:T(8,128)(2,1)S(1)} %constant_dynamic-update-slice_fusion), channel_id=1, source_target_pairs={{0,96},{32,0},{64,32},{96,64},{1,97},{33,1},{65,33},{97,65},{2,98}... | collective-permute-start | bytes 786440 | tf_op jit(solution)/shard_map/ppermute | solution.py:253
  56.6 28.0 %all-to-all-start.1 = ((bf16[256,4,256]{2,1,0:T(4,128)(2,1)}), bf16[256,4,256]{2,1,0:T(4,128)(2,1)S(1)}, u32[]{:S(2)}, u32[]{:S(2)}) async-start(bf16[256,4,256]{2,1,0:T(4,128)(2,1)} %get-tuple-element.18), calls=%async_computation.1 | async-start | bytes 1048576 | tf_op jit(solution)/shard_map/all_to_all | solution.py:248
  63.2 12.6 %copy-start.2 = (bf16[4096,512]{1,0:T(8,128)(2,1)S(1)}, bf16[4096,512]{1,0:T(8,128)(2,1)}, u32[]{:S(2)}) copy-start(bf16[4096,512]{1,0:T(8,128)(2,1)} %copy-done.1) | copy-start | bytes 12582916
  63.2 9.9 %collective-permute-start.3 = (bf16[256,512]{1,0:T(8,128)(2,1)S(1)}, bf16[256,512]{1,0:T(8,128)(2,1)S(1)}, u32[]{:S(2)}, u32[]{:S(2)}) collective-permute-start(bf16[256,512]{1,0:T(8,128)(2,1)S(1)} %constant_dynamic-update-slice_fusion), channel_id=1, source_target_pairs={{0,32},{32,64},{64,96},{96,0},{1,33},{33,65},{65,97},{97,1},{2,34}... | collective-permute-start | bytes 786440 | tf_op jit(solution)/shard_map/ppermute | solution.py:253
  64.7 9.8 %collective-permute-start.6 = (bf16[256,512]{1,0:T(8,128)(2,1)S(1)}, bf16[256,512]{1,0:T(8,128)(2,1)S(1)}, u32[]{:S(2)}, u32[]{:S(2)}) collective-permute-start(bf16[256,512]{1,0:T(8,128)(2,1)S(1)} %constant_dynamic-update-slice_fusion), channel_id=1, source_target_pairs={{0,2},{2,0},{1,3},{3,1},{4,6},{6,4},{5,7},{7,5},{8,10},{10,8},{9,1... | collective-permute-start | bytes 786440 | tf_op jit(solution)/shard_map/ppermute | solution.py:254
  65.5 14.0 %collective-permute-start.8 = (bf16[256,512]{1,0:T(8,128)(2,1)S(1)}, bf16[256,512]{1,0:T(8,128)(2,1)S(1)}, u32[]{:S(2)}, u32[]{:S(2)}) collective-permute-start(bf16[256,512]{1,0:T(8,128)(2,1)S(1)} %collective-permute-done.4), channel_id=1, source_target_pairs={{0,2},{2,0},{1,3},{3,1},{4,6},{6,4},{5,7},{7,5},{8,10},{10,8},{9,1... | collective-permute-start | bytes 786440 | tf_op jit(solution)/shard_map/ppermute | solution.py:254
  68.4 11.4 %collective-permute-start.9 = (bf16[256,512]{1,0:T(8,128)(2,1)S(1)}, bf16[256,512]{1,0:T(8,128)(2,1)S(1)}, u32[]{:S(2)}, u32[]{:S(2)}) collective-permute-start(bf16[256,512]{1,0:T(8,128)(2,1)S(1)} %collective-permute-done.5), channel_id=1, source_target_pairs={{0,2},{2,0},{1,3},{3,1},{4,6},{6,4},{5,7},{7,5},{8,10},{10,8},{9,1... | collective-permute-start | bytes 786440 | tf_op jit(solution)/shard_map/ppermute | solution.py:254
  76.1 4.5 %collective-permute-start.7 = (bf16[256,512]{1,0:T(8,128)(2,1)S(1)}, bf16[256,512]{1,0:T(8,128)(2,1)S(1)}, u32[]{:S(2)}, u32[]{:S(2)}) collective-permute-start(bf16[256,512]{1,0:T(8,128)(2,1)S(1)} %collective-permute-done.3), channel_id=1, source_target_pairs={{0,2},{2,0},{1,3},{3,1},{4,6},{6,4},{5,7},{7,5},{8,10},{10,8},{9,1... | collective-permute-start | bytes 786440 | tf_op jit(solution)/shard_map/ppermute | solution.py:254
  80.1 5.4 %copy-start.5 = (bf16[4,256,128]{2,1,0:T(8,128)(2,1)S(1)}, bf16[4,256,128]{2,1,0:T(8,128)(2,1)}, u32[]{:S(2)}) copy-start(bf16[4,256,128]{2,1,0:T(8,128)(2,1)} %state_ref.1) | copy-start | bytes 786436
  80.1 5.4 %copy-start.6 = (f32[1024,128]{1,0:T(8,128)S(1)}, f32[1024,128]{1,0:T(8,128)}, u32[]{:S(2)}) copy-start(f32[1024,128]{1,0:T(8,128)} %gates.1) | copy-start | bytes 1572868

commit v2 on v1

v2 whole, which is shorter than its diff:
```python
import functools

import jax
import jax.numpy as jnp
from jax import lax
from jax.experimental import pallas as pl
from jax.experimental.pallas import tpu as pltpu
from jax.sharding import Mesh, PartitionSpec as P

FACTOR_WIDTH = 32
ALIGNMENT_ROWS = 128
VMEM_LIMIT = 56 * 1024 * 1024
SMALL_LIMIT = 16 * 1024 * 1024
DEV = ("xl", "y", "z", "c")
PLANE = ("xl", "y", "c", "xh")
ALL = ("xl", "y", "z", "c", "xh")


def apply_layer_norm(values, axis):
    center = jnp.mean(values, axis=axis, keepdims=True)
    spread = jnp.mean((values - center) ** 2, axis=axis, keepdims=True)
    return (values - center) * lax.rsqrt(spread + 1e-05)


def normalize(values):
    values = values - jnp.mean(values, axis=-1, keepdims=True)
    spread = jnp.mean(values * values, axis=-1, keepdims=True)
    return values * lax.rsqrt(spread + 1e-05)


def prepare_kernel(
    grid, state_ref, mask_ref, align_ref, align_mask_ref, weight_ref, align_weight_ref, send_ref, first_ref
):
    rows, half, width = state_ref.shape
    seqs, tokens, _ = align_ref.shape
    align = jnp.swapaxes(align_ref[...].astype(jnp.float32), 0, 1)
    columns = [normalize(align[tok]) for tok in range(tokens)]
    both = lax.dot_general(
        align_weight_ref[...],
        jnp.concatenate(columns, 0).astype(jnp.bfloat16),
        (((0,), (1,)), ((), ())),
        preferred_element_type=jnp.float32,
    )
    align_mask = align_mask_ref[...].astype(jnp.float32)
    tiles = []
    for tok in range(tokens):
        part = both[:, tok * seqs : (tok + 1) * seqs] * align_mask[tok : tok + 1, :]
        first_ref[:, tok * seqs : (tok + 1) * seqs] = part[:FACTOR_WIDTH].astype(jnp.bfloat16)
        part = part[FACTOR_WIDTH:]
        tiles.append(jnp.concatenate([part[: FACTOR_WIDTH // 2], part[FACTOR_WIDTH // 2 :]], 1))
    nx, ny, nz, nc = grid
    pieces = jnp.swapaxes(jnp.stack(tiles), 0, 1).reshape(ny, nx, 1, nc, tokens, 2 * seqs)
    pieces = jnp.broadcast_to(jnp.swapaxes(pieces, 0, 1), (nx, ny, nz, nc, tokens, 2 * seqs))
    send_ref[:, :, 2 * half :] = pieces.reshape(nx * ny * nz * nc, tokens, 2 * seqs).astype(jnp.bfloat16)

    weight = weight_ref[:, : 4 * width]
    factors = []
    for row in range(rows):
        normed = normalize(state_ref[row].astype(jnp.float32)).astype(jnp.bfloat16)
        stacked = lax.dot_general(
            weight, normed, (((0,), (1,)), ((), ())), preferred_element_type=jnp.float32
        )
        maskf = mask_ref[row : row + 1, :].astype(jnp.float32)
        sides = []
        for side in range(2):
            opened = stacked[2 * side * width : (2 * side + 1) * width]
            linear = stacked[(2 * side + 1) * width : (2 * side + 2) * width]
            sides.append(jax.nn.sigmoid(opened) * linear * maskf)
        factors.append(jnp.concatenate(sides, 1))
    send_ref[:, :, : 2 * half] = jnp.swapaxes(jnp.stack(factors), 0, 1).astype(jnp.bfloat16)


def prepare(grid, pair_state, mask, align, align_mask, weight, align_weight):
    rows, half, width = pair_state.shape
    seqs, tokens, _ = align.shape
    return pl.pallas_call(
        functools.partial(prepare_kernel, grid),
        out_shape=(
            jax.ShapeDtypeStruct((width, rows, 2 * half + 2 * seqs), jnp.bfloat16),
            jax.ShapeDtypeStruct((FACTOR_WIDTH, tokens * seqs), jnp.bfloat16),
        ),
        compiler_params=pltpu.CompilerParams(vmem_limit_bytes=VMEM_LIMIT),
        name="prepare",
    )(pair_state, mask, align, align_mask.T, weight, align_weight)


def gate_kernel(state_ref, weight_ref, out_ref):
    values = state_ref[...].astype(jnp.float32)
    values = values - jnp.mean(values, axis=-1, keepdims=True)
    spread = jnp.mean(values * values, axis=-1, keepdims=True)
    normed = (values * lax.rsqrt(spread + 1e-05)).astype(jnp.bfloat16)
    out_ref[...] = jax.nn.sigmoid(
        jnp.dot(normed, weight_ref[:, 4 * state_ref.shape[1] :], preferred_element_type=jnp.float32)
    )


def gates(state, weight):
    return pl.pallas_call(
        gate_kernel,
        out_shape=jax.ShapeDtypeStruct(state.shape, jnp.float32),
        name="gates",
    )(state, weight)


def terms_kernel(place_ref, first_ref, weight_ref, out_ref):
    cores, ny = 2, 4
    width = weight_ref.shape[1]
    rows = out_ref.shape[1] // width // cores
    columns = first_ref.shape[1] // 2 // cores
    seqs = columns // rows
    spread = first_ref[...]
    for turn in range(ny):
        for flip in range(2):
            piece = lax.rem(place_ref[0] + ny - turn, ny) * 2 + lax.rem(place_ref[3] + flip, 2)
            piece = piece * cores + place_ref[1]
            pair = [
                weight_ref[pl.ds((dh * FACTOR_WIDTH // 2 + piece) * FACTOR_WIDTH, FACTOR_WIDTH), :]
                for dh in range(2)
            ]
            product = lax.dot_general(
                spread, jnp.concatenate(pair, 1), (((0,), (0,)), ((), ())), preferred_element_type=jnp.float32
            ).astype(jnp.bfloat16)
            for core in range(cores):
                for other in range(2):
                    for row in range(rows):
                        start = (core * 2 + other) * columns + row * seqs
                        place = (core * rows + row) * width
                        for dh in range(2):
                            at = (((turn * 2 + other) * 2 + flip) * 2 + dh) * seqs
                            out_ref[at : at + seqs, place : place + width] = product[
                                start : start + seqs, dh * width : (dh + 1) * width
                            ]


def outer_terms(place, first, weight, rows):
    columns = first.shape[1]
    depth = FACTOR_WIDTH * columns // rows // 4
    width = weight.shape[1]
    return pl.pallas_call(
        terms_kernel,
        in_specs=[
            pl.BlockSpec(memory_space=pltpu.SMEM),
            pl.BlockSpec(memory_space=pltpu.VMEM),
            pl.BlockSpec(memory_space=pltpu.VMEM),
        ],
        out_shape=jax.ShapeDtypeStruct((depth, 2 * rows * width), jnp.bfloat16),
        cost_estimate=pl.CostEstimate(
            flops=4 * depth * rows * width * FACTOR_WIDTH, bytes_accessed=4 * depth * rows * width, transcendentals=0
        ),
        compiler_params=pltpu.CompilerParams(vmem_limit_bytes=VMEM_LIMIT),
        name="outer_terms",
    )(place, first, weight)


def outer_kernel(*refs):
    *turn_refs, terms_hbm, out_ref, terms_ref, sems = refs
    depth = turn_refs[0].shape[1]
    copies = []
    for index in range(len(turn_refs)):
        rows = pl.ds(index * depth, depth)
        copies.append(pltpu.make_async_copy(terms_hbm.at[rows], terms_ref.at[rows], sems.at[index]))
        copies[-1].start()
    total = 0.0
    for index, ref in enumerate(turn_refs):
        copies[index].wait()
        total = total + jnp.dot(
            ref[...], terms_ref[index * depth : (index + 1) * depth, :], preferred_element_type=jnp.float32
        )
    out_ref[...] = total


def outer_products(turns, terms):
    columns, depth = turns[0].shape
    width = terms.shape[1]
    vmem, hbm = pl.BlockSpec(memory_space=pltpu.VMEM), pl.BlockSpec(memory_space=pl.ANY)
    count = len(turns)
    return pl.pallas_call(
        outer_kernel,
        in_specs=[vmem] * count + [hbm],
        out_shape=jax.ShapeDtypeStruct((columns, width), jnp.float32),
        scratch_shapes=[pltpu.VMEM((count * depth, width), jnp.bfloat16), pltpu.SemaphoreType.DMA((count,))],
        cost_estimate=pl.CostEstimate(
            flops=2 * columns * depth * count * width,
            bytes_accessed=2 * depth * count * (width + columns) + 4 * columns * width,
            transcendentals=0,
        ),
        compiler_params=pltpu.CompilerParams(vmem_limit_bytes=SMALL_LIMIT),
        name="outer_products",
    )(*turns, terms)


def compact(values):
    groups, rows, lanes = values.shape
    pairs = values.reshape(groups // 2, 2, rows, lanes)
    return jnp.concatenate([pairs[:, 0], pairs[:, 1]], 1).reshape(groups * rows, lanes)


def partial_kernel(place_ref, swapped_ref, out_ref, own_ref, away_ref):
    devs, rows, lanes = swapped_ref.shape
    parts = 2
    half = out_ref.shape[2]
    values = compact(swapped_ref[...].astype(jnp.float32))
    left = values[:, :half].astype(jnp.bfloat16)
    right = values[:, half : 2 * half].astype(jnp.bfloat16)
    for part in range(parts):
        product = lax.dot_general(
            left,
            right[part * half : (part + 1) * half],
            (((1,), (1,)), ((), ())),
            preferred_element_type=jnp.float32,
        )
        product = product.reshape(devs // 2, 2 * rows, half)
        product = jnp.stack([product[:, :rows], product[:, rows:]], 1).reshape(devs, rows, half)
        out_ref[part * devs : (part + 1) * devs] = product.astype(jnp.bfloat16)
    table = values[:, 2 * half :].astype(jnp.bfloat16)
    mine = place_ref[2] == 0
    own_ref[...] = jnp.where(mine, table[:half], table[half:])
    away_ref[...] = jnp.where(mine, table[half:], table[:half])


def partials(place, swapped, half):
    devs, rows, lanes = swapped.shape
    table = jax.ShapeDtypeStruct((half, lanes - 2 * half), jnp.bfloat16)
    return pl.pallas_call(
        partial_kernel,
        in_specs=[pl.BlockSpec(memory_space=pltpu.SMEM), pl.BlockSpec(memory_space=pltpu.VMEM)],
        out_shape=(jax.ShapeDtypeStruct((2 * devs, rows, half), jnp.bfloat16), table, table),
        compiler_params=pltpu.CompilerParams(vmem_limit_bytes=SMALL_LIMIT),
        name="partials",
    )(place, swapped)


def merge_kernel(*refs):
    *part_refs, out_ref = refs
    depth = part_refs[0].shape[1]
    for index, ref in enumerate(part_refs):
        out_ref[:, index * depth : (index + 1) * depth] = ref[...]


def merge(*parts):
    columns, depth = parts[0].shape
    return pl.pallas_call(
        merge_kernel,
        out_shape=jax.ShapeDtypeStruct((columns, depth * len(parts)), jnp.bfloat16),
        compiler_params=pltpu.CompilerParams(vmem_limit_bytes=SMALL_LIMIT),
        name="merge",
    )(*parts)


def shards(
    pair_state,
    token_pair_mask,
    alignment_state,
    alignment_mask,
    input_weight,
    output_weight,
    alignment_weight,
    outer_weight,
):
    rows, half, width = pair_state.shape
    points = rows * half
    sizes = [lax.axis_size(name) for name in ALL]
    nx, ny, nz, nc, nr = sizes
    seqs = alignment_state.shape[0]
    devs = nx * ny * nz * nc
    place = jnp.stack([lax.axis_index(name) for name in ("y", "c", "xh", "xl")]).astype(jnp.int32)

    send, fac_a = prepare(
        (nx, ny, nz, nc), pair_state, token_pair_mask, alignment_state, alignment_mask, input_weight, alignment_weight
    )
    swap = [(0, 1), (1, 0)]
    came_a = lax.ppermute(fac_a, "xh", swap)
    swapped = lax.all_to_all(send, DEV, split_axis=0, concat_axis=0, tiled=True)
    both_a = jnp.concatenate([fac_a, came_a], 1)
    both_a = jnp.concatenate([both_a, lax.ppermute(both_a, "c", swap)], 1)
    terms = outer_terms(place, both_a, outer_weight, rows)
    state = pair_state.reshape(points, width)
    gate = gates(state, input_weight)
    swapped, terms, gate = lax.optimization_barrier((swapped, terms, gate))
    partial, own, away = partials(place, swapped, half)
    back = lax.all_to_all(partial, ("xh",) + DEV, split_axis=0, concat_axis=0, tiled=True)

    table = [
        own,
        lax.ppermute(own, "xl", swap),
        lax.ppermute(away, "xh", swap),
        lax.ppermute(away, ("xl", "xh"), [(0, 3), (1, 2), (2, 1), (3, 0)]),
    ]
    turns = [jnp.concatenate(table, 1)]
    for turn in range(1, ny):
        turns.append(lax.ppermute(turns[0], "y", [(i, (i + turn) % ny) for i in range(ny)]))
    depth = turns[0].shape[1]
    opm = outer_products(turns[:2], terms)
    for index in range(2, ny):
        opm = opm + jnp.dot(
            turns[index], terms[index * depth : (index + 1) * depth], preferred_element_type=jnp.float32
        )
    opm = opm * (1.0 / ALIGNMENT_ROWS)
    opm, other = opm[:, : rows * width], opm[:, rows * width :].astype(jnp.bfloat16)
    other, back = lax.optimization_barrier((other, back))
    other = lax.ppermute(other, "c", swap)

    back = back.reshape(nr, devs, points).astype(jnp.float32)
    tri_sum = (back[0] + back[1]).astype(jnp.bfloat16).astype(jnp.float32)
    tri_norm = apply_layer_norm(tri_sum, 0).astype(jnp.bfloat16)
    tri_out = gate * jnp.einsum(
        "cp,cd->pd", tri_norm, output_weight, preferred_element_type=jnp.float32
    )
    opm = (opm + other.astype(jnp.float32)).reshape(half, rows, width)
    opm = jnp.transpose(opm, (1, 0, 2)).reshape(points, width)
    return (state.astype(jnp.float32) + opm + tri_out).astype(jnp.bfloat16).reshape(rows, half, width)


def solution(mesh):
    grid = Mesh(mesh.devices.reshape(2, 4, 8, 2, 2), ALL)
    inner = jax.shard_map(
        shards,
        mesh=grid,
        in_specs=(
            P(DEV, "xh", None),
            P(DEV, "xh"),
            P("xh", DEV, None),
            P("xh", DEV),
            P(),
            P(),
            P(),
            P(),
        ),
        out_specs=P(DEV, "xh", None),
        check_vma=False,
    )
    return inner
```

time: 86.9 us -> 80.7 us (0.929)
  matrix products: 6.81 us -> 1.85 us
  starting transfers between devices: 39.6 us -> 37.9 us
  waiting for transfers between devices: 23.4 us -> 21.9 us
  Pallas kernels: 11 us -> 12.4 us
  other arithmetic: 2.17 us -> 3.38 us
    ppermute x3, waiting for transfers between devices: 2.71 us -> 11.3 us  [shards(): lax.ppermute(turns[0], 'y', [(i, (i + turn) % ny) for i in range(ny)])]
    all_to_all x1, waiting for transfers between devices: 12.4 us -> 5.4 us  [shards(): swapped = lax.all_to_all(send, DEV, split_axis=0, concat_axis=0, tiled=True)]
    dot_general x8 -> x2, matrix products: 6.54 us -> 0.88 us  [shards(): jnp.dot(turns[index], terms[index * depth:(index + 1) * depth], preferred...]
    all_to_all x1, waiting for transfers between devices: 3.59 us -> 0.01 us  [shards(): lax.all_to_all(partial, ('xh',) + DEV, split_axis=0, concat_axis=0, tiled...]
    pallas_call x1, Pallas kernels: 1.82 us -> 4.36 us  [outer_terms(): pl.pallas_call(terms_kernel, in_specs=[pl.BlockSpec(memory_space=pltpu.SM...]
    ppermute x1, waiting for transfers between devices: 0.08 us -> 2.33 us  [shards(): came_a = lax.ppermute(fac_a, 'xh', swap)]
    concatenate x1 -> x2, other arithmetic: 0.01 us -> 2.07 us  [the longest x1 1.35 us: shards(): both_a = jnp.concatenate([both_a, lax.ppermute(both_a, 'c', swap)], 1)]
    all_to_all x1, starting transfers between devices: 16.9 us -> 14.9 us  [shards(): swapped = lax.all_to_all(send, DEV, split_axis=0, concat_axis=0, tiled=True)]
  transfers between devices with their start and end apart: 12 -> 11, of which waited for: 7 -> 6; matrix products, arithmetic and copies ran while one was open for 9% -> 5% of each run, Pallas kernels for 8% -> 9%
where the time goes in v2:
time: 80.7 us; the launch traced here: 80.3 us
  starting transfers between devices  37.9 us (47%)
  waiting for transfers between devices  21.9 us (27%)
  Pallas kernels  12.4 us (15%)
  other arithmetic  3.38 us (4%)
  local copies, waits for them, and re-layouts  2.63 us (3%)
  matrix products  1.85 us (2%)
    all_to_all x1, starting transfers between devices, shards(): swapped = lax.all_to_all(send, DEV, split_axis=0, concat_axis=0, tiled=True)  14.9 us
    ppermute x3, waiting for transfers between devices, shards(): lax.ppermute(turns[0], 'y', [(i, (i + turn) % ny) for i in range(ny)])  11.3 us
    all_to_all x1, starting transfers between devices, shards(): lax.all_to_all(partial, ('xh',) + DEV, split_axis=0, concat_axis=0, tiled...  8.53 us
    all_to_all x1, waiting for transfers between devices, shards(): swapped = lax.all_to_all(send, DEV, split_axis=0, concat_axis=0, tiled=True)  5.4 us
    ppermute x3, starting transfers between devices, shards(): lax.ppermute(turns[0], 'y', [(i, (i + turn) % ny) for i in range(ny)])  5.22 us
    pallas_call x1, Pallas kernels, outer_terms(): pl.pallas_call(terms_kernel, in_specs=[pl.BlockSpec(memory_space=pltpu.SM...  4.36 us
    pallas_call x1, Pallas kernels, prepare(): pl.pallas_call(functools.partial(prepare_kernel, grid), out_shape=(jax.Sh...  3.08 us
    ppermute x1, starting transfers between devices, shards(): came_a = lax.ppermute(fac_a, 'xh', swap)  2.54 us
  transfers between devices with their start and end apart: 11, of which 6 were waited for; matrix products, arithmetic and copies ran while one was open for 5% of the time, Pallas kernels for 9%

profile of v2, /device:TPU:1, one launch (start us, length us, event | category | flops | bytes accessed | tf_op | source)
XLA Modules:
  0.0 80.3 jit_solution(862310302682539677)
XLA Ops:
  0.0 0.0 copy-start
  0.0 3.1 %prepare.1 = (bf16[128,4,640]{2,1,0:T(4,128)(2,1)}, bf16[32,256]{1,0:T(8,128)(2,1)}) custom-call(bf16[4,256,128]{2,1,0:T(8,128)(2,1)} %state_ref.1, s32[4,256]{1,0:T(4,128)} %mask_ref.1, bf16[64,4,64]{2,1,0:T(4,128)(2,1)} %align_ref.1, s32[4,64]{1,0:T(4,128)} %bitcast.26, bf16[128,640]{1,0:T(8,128)(2,1)} %weight_ref.5, bf16[64,64]{1,0:T(8,128)(2,1)} %align_weight_ref.1), custom_call_target="tpu_custom_call" | custom-call | tf_op jit(solution)/shard_map/prepare/pallas_call | solution.py:76
  3.1 14.9 %all-to-all-start = ((bf16[128,4,640]{2,1,0:T(4,128)(2,1)}), bf16[128,4,640]{2,1,0:T(4,128)(2,1)S(1)}, u32[]{:S(2)}, u32[]{:S(2)}) async-start(bf16[128,4,640]{2,1,0:T(4,128)(2,1)} %get-tuple-element.15), calls=%async_computation | async-start | bytes 1310720 | tf_op jit(solution)/shard_map/all_to_all | solution.py:273
  18.0 2.5 %collective-permute-start = (bf16[32,256]{1,0:T(8,128)(2,1)}, bf16[32,256]{1,0:T(8,128)(2,1)S(1)}, u32[]{:S(2)}, u32[]{:S(2)}) collective-permute-start(bf16[32,256]{1,0:T(8,128)(2,1)} %get-tuple-element.16), channel_id=1, source_target_pairs={{0,1},{1,0},{2,3},{3,2},{4,5},{5,4},{6,7},{7,6},{8,9},{9,8},{10,11... | collective-permute-start | bytes 49160 | tf_op jit(solution)/shard_map/ppermute | solution.py:272
  20.5 2.3 %collective-permute-done = bf16[32,256]{1,0:T(8,128)(2,1)S(1)} collective-permute-done((bf16[32,256]{1,0:T(8,128)(2,1)}, bf16[32,256]{1,0:T(8,128)(2,1)S(1)}, u32[]{:S(2)}, u32[]{:S(2)}) %collective-permute-start) | collective-permute-done | bytes 16416 | tf_op jit(solution)/shard_map/ppermute | solution.py:272
  22.8 0.7 pad_maximum_fusion.1
  23.6 1.6 %collective-permute-start.1 = (bf16[32,512]{1,0:T(8,128)(2,1)S(1)}, bf16[32,512]{1,0:T(8,128)(2,1)S(1)}, u32[]{:S(2)}, u32[]{:S(2)}) collective-permute-start(bf16[32,512]{1,0:T(8,128)(2,1)S(1)} %pad_maximum_fusion.1), channel_id=1, source_target_pairs={{0,2},{2,0},{1,3},{3,1},{4,6},{6,4},{5,7},{7,5},{8,10},{10,8},{9,1... | collective-permute-start | bytes 98312 | tf_op jit(solution)/shard_map/ppermute | solution.py:275
  25.1 0.7 pad_add_fusion.place_ref
  25.8 0.0 copy-start.2
  25.8 2.3 %gates.1 = f32[1024,128]{1,0:T(8,128)} custom-call(bf16[1024,128]{1,0:T(8,128)(2,1)} %bitcast.21, bf16[128,640]{1,0:T(8,128)(2,1)} %weight_ref.5), custom_call_target="tpu_custom_call" | custom-call | tf_op jit(solution)/shard_map/gates/pallas_call | solution.py:98
  28.0 0.0 collective-permute-done.1
  28.0 1.4 %pad_maximum_fusion.first_ref = bf16[32,1024]{1,0:T(8,128)(2,1)} fusion(bf16[32,512]{1,0:T(8,128)(2,1)S(1)} %collective-permute-done.1, bf16[32,256]{1,0:T(8,128)(2,1)S(1)} %collective-permute-done, bf16[32,256]{1,0:T(8,128)(2,1)} %get-tuple-element.16), kind=kLoop, calls=%fused_computation.18 | loop fusion | flops 196608 | bytes 131072 | tf_op jit(solution)/shard_map/concatenate | solution.py:275
  29.4 4.4 %outer_terms.1.refs_2_ = bf16[2048,1024]{1,0:T(8,128)(2,1)} custom-call(s32[4]{0:T(128)} %pad_add_fusion.place_ref, bf16[32,1024]{1,0:T(8,128)(2,1)} %pad_maximum_fusion.first_ref, bf16[1024,128]{1,0:T(8,128)(2,1)} %weight_ref.4), custom_call_target="tpu_custom_call" | custom-call | flops 134217728 | bytes 4194304 | tf_op jit(solution)/shard_map/outer_terms/pallas_call | solution.py:139
  33.8 5.4 %all-to-all-done.swapped_ref = bf16[128,4,640]{2,1,0:T(4,128)(2,1)S(1)} async-done(((bf16[128,4,640]{2,1,0:T(4,128)(2,1)}), bf16[128,4,640]{2,1,0:T(4,128)(2,1)S(1)}, u32[]{:S(2)}, u32[]{:S(2)}) %all-to-all-start) | async-done | bytes 655392 | tf_op jit(solution)/shard_map/all_to_all | solution.py:273
  39.2 0.0 copy-done.2
  39.2 1.7 %partials.1 = (bf16[256,4,256]{2,1,0:T(4,128)(2,1)}, bf16[256,128]{1,0:T(8,128)(2,1)S(1)}, bf16[256,128]{1,0:T(8,128)(2,1)S(1)}) custom-call(s32[4]{0:T(128)S(1)} %copy-done.2, bf16[128,4,640]{2,1,0:T(4,128)(2,1)S(1)} %all-to-all-done.swapped_ref), custom_call_target="tpu_custom_call" | custom-call | tf_op jit(solution)/shard_map/partials/pallas_call | solution.py:224
  40.9 1.8 %collective-permute-start.4 = (bf16[256,128]{1,0:T(8,128)(2,1)S(1)}, bf16[256,128]{1,0:T(8,128)(2,1)S(1)}, u32[]{:S(2)}, u32[]{:S(2)}) collective-permute-start(bf16[256,128]{1,0:T(8,128)(2,1)S(1)} %get-tuple-element.19), channel_id=1, source_target_pairs={{0,129},{1,128},{128,1},{129,0},{2,131},{3,130},{130,3},{131,2},{4... | collective-permute-start | bytes 196616 | tf_op jit(solution)/shard_map/ppermute | solution.py:287
  42.7 0.7 collective-permute-start.3
  43.3 8.5 %all-to-all-start.1 = ((bf16[256,4,256]{2,1,0:T(4,128)(2,1)}), bf16[256,4,256]{2,1,0:T(4,128)(2,1)S(1)}, u32[]{:S(2)}, u32[]{:S(2)}) async-start(bf16[256,4,256]{2,1,0:T(4,128)(2,1)} %get-tuple-element.21), calls=%async_computation.1 | async-start | bytes 1048576 | tf_op jit(solution)/shard_map/all_to_all | solution.py:281
  51.9 1.5 %collective-permute-start.2 = (bf16[256,128]{1,0:T(8,128)(2,1)S(1)}, bf16[256,128]{1,0:T(8,128)(2,1)S(1)}, u32[]{:S(2)}, u32[]{:S(2)}) collective-permute-start(bf16[256,128]{1,0:T(8,128)(2,1)S(1)} %get-tuple-element.18), channel_id=1, source_target_pairs={{0,128},{128,0},{1,129},{129,1},{2,130},{130,2},{3,131},{131,3},{4... | collective-permute-start | bytes 196616 | tf_op jit(solution)/shard_map/ppermute | solution.py:285
  53.4 2.3 %collective-permute-done.2 = bf16[256,128]{1,0:T(8,128)(2,1)S(1)} collective-permute-done((bf16[256,128]{1,0:T(8,128)(2,1)S(1)}, bf16[256,128]{1,0:T(8,128)(2,1)S(1)}, u32[]{:S(2)}, u32[]{:S(2)}) %collective-permute-start.2) | collective-permute-done | bytes 65568 | tf_op jit(solution)/shard_map/ppermute | solution.py:285
  55.7 0.0 collective-permute-done.3
  55.8 0.0 collective-permute-done.4
  55.8 1.5 %collective-permute-start.5 = (bf16[256,512]{1,0:T(8,128)(2,1)S(1)}, bf16[256,512]{1,0:T(8,128)(2,1)S(1)}, u32[]{:S(2)}, u32[]{:S(2)}) collective-permute-start(bf16[256,512]{1,0:T(8,128)(2,1)S(1)} %constant_dynamic-update-slice_fusion.refs_0_), channel_id=1, source_target_pairs={{0,32},{32,64},{64,96},{96,0},{1,33},{33,65},{65,97},{97,1},{2,34}... | collective-permute-start | bytes 786440 | tf_op jit(solution)/shard_map/ppermute | solution.py:291
  57.3 2.5 %collective-permute-start.6 = (bf16[256,512]{1,0:T(8,128)(2,1)S(1)}, bf16[256,512]{1,0:T(8,128)(2,1)S(1)}, u32[]{:S(2)}, u32[]{:S(2)}) collective-permute-start(bf16[256,512]{1,0:T(8,128)(2,1)S(1)} %constant_dynamic-update-slice_fusion.refs_0_), channel_id=1, source_target_pairs={{0,64},{32,96},{64,0},{96,32},{1,65},{33,97},{65,1},{97,33},{2,66}... | collective-permute-start | bytes 786440 | tf_op jit(solution)/shard_map/ppermute | solution.py:291
  59.8 1.2 %collective-permute-start.7 = (bf16[256,512]{1,0:T(8,128)(2,1)S(1)}, bf16[256,512]{1,0:T(8,128)(2,1)S(1)}, u32[]{:S(2)}, u32[]{:S(2)}) collective-permute-start(bf16[256,512]{1,0:T(8,128)(2,1)S(1)} %constant_dynamic-update-slice_fusion.refs_0_), channel_id=1, source_target_pairs={{0,96},{32,0},{64,32},{96,64},{1,97},{33,1},{65,33},{97,65},{2,98}... | collective-permute-start | bytes 786440 | tf_op jit(solution)/shard_map/ppermute | solution.py:291
  61.0 5.0 %collective-permute-done.5.refs_1_ = bf16[256,512]{1,0:T(8,128)(2,1)S(1)} collective-permute-done((bf16[256,512]{1,0:T(8,128)(2,1)S(1)}, bf16[256,512]{1,0:T(8,128)(2,1)S(1)}, u32[]{:S(2)}, u32[]{:S(2)}) %collective-permute-start.5) | collective-permute-done | bytes 262176 | tf_op jit(solution)/shard_map/ppermute | solution.py:291
  66.0 0.0 copy-start.1
  66.0 2.2 %copy-done.1 = bf16[2048,1024]{1,0:T(8,128)(2,1)S(1)} copy-done((bf16[2048,1024]{1,0:T(8,128)(2,1)S(1)}, bf16[2048,1024]{1,0:T(8,128)(2,1)}, u32[]{:S(2)}) %copy-start.1) | copy-done | bytes 4194328
  68.2 0.9 %outer_products.1 = f32[256,1024]{1,0:T(8,128)S(1)} custom-call(bf16[256,512]{1,0:T(8,128)(2,1)S(1)} %constant_dynamic-update-slice_fusion.refs_0_, bf16[256,512]{1,0:T(8,128)(2,1)S(1)} %collective-permute-done.5.refs_1_, bf16[2048,1024]{1,0:T(8,128)(2,1)S(1)} %copy-done.1), custom_call_target="tpu_custom_call" | custom-call | flops 536870912 | bytes 3670016 | tf_op jit(solution)/shard_map/outer_products/pallas_call | solution.py:177
  69.2 6.3 %collective-permute-done.6 = bf16[256,512]{1,0:T(8,128)(2,1)S(1)} collective-permute-done((bf16[256,512]{1,0:T(8,128)(2,1)S(1)}, bf16[256,512]{1,0:T(8,128)(2,1)S(1)}, u32[]{:S(2)}, u32[]{:S(2)}) %collective-permute-start.6) | collective-permute-done | bytes 262176 | tf_op jit(solution)/shard_map/ppermute | solution.py:291
  75.5 0.4 fusion.4
  75.9 0.0 collective-permute-done.7
  75.9 0.4 add_multiply_fusion
  76.4 0.0 copy-start.3
  76.4 0.0 all-to-all-done.1
  76.4 1.2 %collective-permute-start.8 = (bf16[256,512]{1,0:T(8,128)(2,1)S(1)}, bf16[256,512]{1,0:T(8,128)(2,1)S(1)}, u32[]{:S(2)}, u32[]{:S(2)}) collective-permute-start(bf16[256,512]{1,0:T(8,128)(2,1)S(1)} %slice.45), channel_id=1, source_target_pairs={{0,2},{2,0},{1,3},{3,1},{4,6},{6,4},{5,7},{7,5},{8,10},{10,8},{9,1... | collective-permute-start | bytes 786440 | tf_op jit(solution)/shard_map/ppermute | solution.py:301
  77.7 0.1 convert_element_type.31
  77.8 0.0 copy-start.4
  77.8 0.3 fusion.10
  78.1 0.1 copy.10
  78.2 0.1 multiply_reduce_fusion
  78.3 0.5 collective-permute-done.8
  78.9 0.1 slice_add_fusion.1
  78.9 0.2 reshape.38
  79.2 0.0 copy-done.3
  79.2 0.1 bitcast_add_fusion
  79.3 0.0 copy-done
  79.3 0.0 copy-done.4
  79.3 1.0 %fusion.1 = bf16[1024,128]{1,0:T(8,128)(2,1)} fusion(f32[1024,128]{1,0:T(8,128)S(1)} %bitcast_add_fusion, f32[1024,128]{1,0:T(8,128)S(1)} %copy-done.4, bf16[128,128]{1,0:T(8,128)(2,1)S(1)} %copy-done, f32[128,1024]{1,0:T(8,128)S(1)} %bitcast.20, f32[1024]{0:T(1024)S(1)} %add_rsqrt_fusion, f32[1024]{0:T(1024)S(1)} %bitcast.25), kind=kOutput, calls=%fused_computation.2 | convolution fusion | flops 34340864 | bytes 1875968 | tf_op jit(solution)/shard_map/cp,cd->pd/dot_general | solution.py:306
  (9 shorter events, 0.2 us)
Async XLA Ops:
  0.0 79.3 %copy-start = (bf16[128,128]{1,0:T(8,128)(2,1)S(1)}, bf16[128,128]{1,0:T(8,128)(2,1)}, u32[]{:S(2)}) copy-start(bf16[128,128]{1,0:T(8,128)(2,1)} %param.13) | copy-start | bytes 98308
  3.1 36.1 %all-to-all-start = ((bf16[128,4,640]{2,1,0:T(4,128)(2,1)}), bf16[128,4,640]{2,1,0:T(4,128)(2,1)S(1)}, u32[]{:S(2)}, u32[]{:S(2)}) async-start(bf16[128,4,640]{2,1,0:T(4,128)(2,1)} %get-tuple-element.15), calls=%async_computation | async-start | bytes 1310720 | tf_op jit(solution)/shard_map/all_to_all | solution.py:273
  18.0 4.9 %collective-permute-start = (bf16[32,256]{1,0:T(8,128)(2,1)}, bf16[32,256]{1,0:T(8,128)(2,1)S(1)}, u32[]{:S(2)}, u32[]{:S(2)}) collective-permute-start(bf16[32,256]{1,0:T(8,128)(2,1)} %get-tuple-element.16), channel_id=1, source_target_pairs={{0,1},{1,0},{2,3},{3,2},{4,5},{5,4},{6,7},{7,6},{8,9},{9,8},{10,11... | collective-permute-start | bytes 49160 | tf_op jit(solution)/shard_map/ppermute | solution.py:272
  23.6 4.5 %collective-permute-start.1 = (bf16[32,512]{1,0:T(8,128)(2,1)S(1)}, bf16[32,512]{1,0:T(8,128)(2,1)S(1)}, u32[]{:S(2)}, u32[]{:S(2)}) collective-permute-start(bf16[32,512]{1,0:T(8,128)(2,1)S(1)} %pad_maximum_fusion.1), channel_id=1, source_target_pairs={{0,2},{2,0},{1,3},{3,1},{4,6},{6,4},{5,7},{7,5},{8,10},{10,8},{9,1... | collective-permute-start | bytes 98312 | tf_op jit(solution)/shard_map/ppermute | solution.py:275
  25.8 13.4 %copy-start.2 = (s32[4]{0:T(128)S(1)}, s32[4]{0:T(128)}, u32[]{:S(2)}) copy-start(s32[4]{0:T(128)} %pad_add_fusion.place_ref) | copy-start | bytes 52
  40.9 14.9 %collective-permute-start.4 = (bf16[256,128]{1,0:T(8,128)(2,1)S(1)}, bf16[256,128]{1,0:T(8,128)(2,1)S(1)}, u32[]{:S(2)}, u32[]{:S(2)}) collective-permute-start(bf16[256,128]{1,0:T(8,128)(2,1)S(1)} %get-tuple-element.19), channel_id=1, source_target_pairs={{0,129},{1,128},{128,1},{129,0},{2,131},{3,130},{130,3},{131,2},{4... | collective-permute-start | bytes 196616 | tf_op jit(solution)/shard_map/ppermute | solution.py:287
  42.7 13.1 %collective-permute-start.3 = (bf16[256,128]{1,0:T(8,128)(2,1)S(1)}, bf16[256,128]{1,0:T(8,128)(2,1)S(1)}, u32[]{:S(2)}, u32[]{:S(2)}) collective-permute-start(bf16[256,128]{1,0:T(8,128)(2,1)S(1)} %get-tuple-element.19), channel_id=1, source_target_pairs={{0,1},{1,0},{2,3},{3,2},{4,5},{5,4},{6,7},{7,6},{8,9},{9,8},{10,11... | collective-permute-start | bytes 196616 | tf_op jit(solution)/shard_map/ppermute | solution.py:286
  43.3 33.1 %all-to-all-start.1 = ((bf16[256,4,256]{2,1,0:T(4,128)(2,1)}), bf16[256,4,256]{2,1,0:T(4,128)(2,1)S(1)}, u32[]{:S(2)}, u32[]{:S(2)}) async-start(bf16[256,4,256]{2,1,0:T(4,128)(2,1)} %get-tuple-element.21), calls=%async_computation.1 | async-start | bytes 1048576 | tf_op jit(solution)/shard_map/all_to_all | solution.py:281
  51.9 3.8 %collective-permute-start.2 = (bf16[256,128]{1,0:T(8,128)(2,1)S(1)}, bf16[256,128]{1,0:T(8,128)(2,1)S(1)}, u32[]{:S(2)}, u32[]{:S(2)}) collective-permute-start(bf16[256,128]{1,0:T(8,128)(2,1)S(1)} %get-tuple-element.18), channel_id=1, source_target_pairs={{0,128},{128,0},{1,129},{129,1},{2,130},{130,2},{3,131},{131,3},{4... | collective-permute-start | bytes 196616 | tf_op jit(solution)/shard_map/ppermute | solution.py:285
  55.8 10.2 %collective-permute-start.5 = (bf16[256,512]{1,0:T(8,128)(2,1)S(1)}, bf16[256,512]{1,0:T(8,128)(2,1)S(1)}, u32[]{:S(2)}, u32[]{:S(2)}) collective-permute-start(bf16[256,512]{1,0:T(8,128)(2,1)S(1)} %constant_dynamic-update-slice_fusion.refs_0_), channel_id=1, source_target_pairs={{0,32},{32,64},{64,96},{96,0},{1,33},{33,65},{65,97},{97,1},{2,34}... | collective-permute-start | bytes 786440 | tf_op jit(solution)/shard_map/ppermute | solution.py:291
  57.3 18.2 %collective-permute-start.6 = (bf16[256,512]{1,0:T(8,128)(2,1)S(1)}, bf16[256,512]{1,0:T(8,128)(2,1)S(1)}, u32[]{:S(2)}, u32[]{:S(2)}) collective-permute-start(bf16[256,512]{1,0:T(8,128)(2,1)S(1)} %constant_dynamic-update-slice_fusion.refs_0_), channel_id=1, source_target_pairs={{0,64},{32,96},{64,0},{96,32},{1,65},{33,97},{65,1},{97,33},{2,66}... | collective-permute-start | bytes 786440 | tf_op jit(solution)/shard_map/ppermute | solution.py:291
  59.8 16.1 %collective-permute-start.7 = (bf16[256,512]{1,0:T(8,128)(2,1)S(1)}, bf16[256,512]{1,0:T(8,128)(2,1)S(1)}, u32[]{:S(2)}, u32[]{:S(2)}) collective-permute-start(bf16[256,512]{1,0:T(8,128)(2,1)S(1)} %constant_dynamic-update-slice_fusion.refs_0_), channel_id=1, source_target_pairs={{0,96},{32,0},{64,32},{96,64},{1,97},{33,1},{65,33},{97,65},{2,98}... | collective-permute-start | bytes 786440 | tf_op jit(solution)/shard_map/ppermute | solution.py:291
  66.0 2.2 %copy-start.1 = (bf16[2048,1024]{1,0:T(8,128)(2,1)S(1)}, bf16[2048,1024]{1,0:T(8,128)(2,1)}, u32[]{:S(2)}) copy-start(bf16[2048,1024]{1,0:T(8,128)(2,1)} %outer_terms.1.refs_2_) | copy-start | bytes 12582916
  76.4 2.8 %copy-start.3 = (bf16[4,256,128]{2,1,0:T(8,128)(2,1)S(1)}, bf16[4,256,128]{2,1,0:T(8,128)(2,1)}, u32[]{:S(2)}) copy-start(bf16[4,256,128]{2,1,0:T(8,128)(2,1)} %state_ref.1) | copy-start | bytes 786436
  76.4 2.4 %collective-permute-start.8 = (bf16[256,512]{1,0:T(8,128)(2,1)S(1)}, bf16[256,512]{1,0:T(8,128)(2,1)S(1)}, u32[]{:S(2)}, u32[]{:S(2)}) collective-permute-start(bf16[256,512]{1,0:T(8,128)(2,1)S(1)} %slice.45), channel_id=1, source_target_pairs={{0,2},{2,0},{1,3},{3,1},{4,6},{6,4},{5,7},{7,5},{8,10},{10,8},{9,1... | collective-permute-start | bytes 786440 | tf_op jit(solution)/shard_map/ppermute | solution.py:301
  77.8 1.4 %copy-start.4 = (f32[1024,128]{1,0:T(8,128)S(1)}, f32[1024,128]{1,0:T(8,128)}, u32[]{:S(2)}) copy-start(f32[1024,128]{1,0:T(8,128)} %gates.1) | copy-start | bytes 1572868

commit v3 on v2

--- a/solution.py
+++ b/solution.py
@@ -11,6 +11,7 @@
 ALIGNMENT_ROWS = 128
 VMEM_LIMIT = 56 * 1024 * 1024
 SMALL_LIMIT = 16 * 1024 * 1024
+TURNS = (0, 2, 1, 3)
 DEV = ("xl", "y", "z", "c")
 PLANE = ("xl", "y", "c", "xh")
 ALL = ("xl", "y", "z", "c", "xh")
@@ -102,16 +103,22 @@
     )(state, weight)
 
 
-def terms_kernel(place_ref, first_ref, weight_ref, out_ref):
+def terms_kernel(place_ref, first_ref, came_ref, weight_ref, out_ref):
     cores, ny = 2, 4
     width = weight_ref.shape[1]
     rows = out_ref.shape[1] // width // cores
-    columns = first_ref.shape[1] // 2 // cores
+    columns = first_ref.shape[1] // cores
     seqs = columns // rows
-    spread = first_ref[...]
-    for turn in range(ny):
+    spread = []
+    for core in range(cores):
+        spread.append(first_ref[:, core * columns : (core + 1) * columns])
+        for pair in range(columns // width):
+            start = (core * columns // width + pair) * FACTOR_WIDTH
+            spread.append(came_ref[start : start + FACTOR_WIDTH, :])
+    spread = jnp.concatenate(spread, 1)
+    for turn, shift in enumerate(TURNS):
         for flip in range(2):
-            piece = lax.rem(place_ref[0] + ny - turn, ny) * 2 + lax.rem(place_ref[3] + flip, 2)
+            piece = lax.rem(place_ref[0] + ny - shift, ny) * 2 + lax.rem(place_ref[3] + flip, 2)
             piece = piece * cores + place_ref[1]
             pair = [
                 weight_ref[pl.ds((dh * FACTOR_WIDTH // 2 + piece) * FACTOR_WIDTH, FACTOR_WIDTH), :]
@@ -126,43 +133,33 @@
                         start = (core * 2 + other) * columns + row * seqs
                         place = (core * rows + row) * width
                         for dh in range(2):
-                            at = (((turn * 2 + other) * 2 + flip) * 2 + dh) * seqs
+                            at = (((flip * ny + turn) * 2 + other) * 2 + dh) * seqs
                             out_ref[at : at + seqs, place : place + width] = product[
                                 start : start + seqs, dh * width : (dh + 1) * width
                             ]
 
 
-def outer_terms(place, first, weight, rows):
-    columns = first.shape[1]
-    depth = FACTOR_WIDTH * columns // rows // 4
+def outer_terms(place, first, came, weight, rows):
+    depth = FACTOR_WIDTH * first.shape[1] // rows // 2
     width = weight.shape[1]
+    vmem = pl.BlockSpec(memory_space=pltpu.VMEM)
     return pl.pallas_call(
         terms_kernel,
-        in_specs=[
-            pl.BlockSpec(memory_space=pltpu.SMEM),
-            pl.BlockSpec(memory_space=pltpu.VMEM),
-            pl.BlockSpec(memory_space=pltpu.VMEM),
-        ],
+        in_specs=[pl.BlockSpec(memory_space=pltpu.SMEM), vmem, vmem, vmem],
         out_shape=jax.ShapeDtypeStruct((depth, 2 * rows * width), jnp.bfloat16),
         cost_estimate=pl.CostEstimate(
             flops=4 * depth * rows * width * FACTOR_WIDTH, bytes_accessed=4 * depth * rows * width, transcendentals=0
         ),
-        compiler_params=pltpu.CompilerParams(vmem_limit_bytes=VMEM_LIMIT),
+        compiler_params=pltpu.CompilerParams(vmem_limit_bytes=SMALL_LIMIT),
         name="outer_terms",
-    )(place, first, weight)
+    )(place, first, came, weight)
 
 
 def outer_kernel(*refs):
-    *turn_refs, terms_hbm, out_ref, terms_ref, sems = refs
+    *turn_refs, terms_ref, out_ref = refs
     depth = turn_refs[0].shape[1]
-    copies = []
-    for index in range(len(turn_refs)):
-        rows = pl.ds(index * depth, depth)
-        copies.append(pltpu.make_async_copy(terms_hbm.at[rows], terms_ref.at[rows], sems.at[index]))
-        copies[-1].start()
     total = 0.0
     for index, ref in enumerate(turn_refs):
-        copies[index].wait()
         total = total + jnp.dot(
             ref[...], terms_ref[index * depth : (index + 1) * depth, :], preferred_element_type=jnp.float32
         )
@@ -172,13 +169,10 @@
 def outer_products(turns, terms):
     columns, depth = turns[0].shape
     width = terms.shape[1]
-    vmem, hbm = pl.BlockSpec(memory_space=pltpu.VMEM), pl.BlockSpec(memory_space=pl.ANY)
     count = len(turns)
     return pl.pallas_call(
         outer_kernel,
-        in_specs=[vmem] * count + [hbm],
         out_shape=jax.ShapeDtypeStruct((columns, width), jnp.float32),
-        scratch_shapes=[pltpu.VMEM((count * depth, width), jnp.bfloat16), pltpu.SemaphoreType.DMA((count,))],
         cost_estimate=pl.CostEstimate(
             flops=2 * columns * depth * count * width,
             bytes_accessed=2 * depth * count * (width + columns) + 4 * columns * width,
@@ -195,7 +189,7 @@
     return jnp.concatenate([pairs[:, 0], pairs[:, 1]], 1).reshape(groups * rows, lanes)
 
 
-def partial_kernel(place_ref, swapped_ref, out_ref, own_ref, away_ref):
+def partial_kernel(flag_ref, swapped_ref, first_ref, out_ref, own_ref, away_ref):
     devs, rows, lanes = swapped_ref.shape
     parts = 2
     half = out_ref.shape[2]
@@ -212,39 +206,29 @@
         product = product.reshape(devs // 2, 2 * rows, half)
         product = jnp.stack([product[:, :rows], product[:, rows:]], 1).reshape(devs, rows, half)
         out_ref[part * devs : (part + 1) * devs] = product.astype(jnp.bfloat16)
-    table = values[:, 2 * half :].astype(jnp.bfloat16)
-    mine = place_ref[2] == 0
-    own_ref[...] = jnp.where(mine, table[:half], table[half:])
-    away_ref[...] = jnp.where(mine, table[half:], table[:half])
-
-
-def partials(place, swapped, half):
+    table = values[:, 2 * half :]
+    mine = flag_ref[0:1, :] > 0.5
+    own_ref[...] = jnp.where(mine, table[:half], table[half:]).astype(jnp.bfloat16)
+    away_ref[:half] = jnp.where(mine, table[half:], table[:half]).astype(jnp.bfloat16)
+    lanes = away_ref.shape[1]
+    for index in range(first_ref.shape[1] // lanes):
+        start = half + index * FACTOR_WIDTH
+        away_ref[start : start + FACTOR_WIDTH] = first_ref[:, index * lanes : (index + 1) * lanes]
+
+
+def partials(flag, swapped, first, half):
     devs, rows, lanes = swapped.shape
-    table = jax.ShapeDtypeStruct((half, lanes - 2 * half), jnp.bfloat16)
+    lanes -= 2 * half
     return pl.pallas_call(
         partial_kernel,
-        in_specs=[pl.BlockSpec(memory_space=pltpu.SMEM), pl.BlockSpec(memory_space=pltpu.VMEM)],
-        out_shape=(jax.ShapeDtypeStruct((2 * devs, rows, half), jnp.bfloat16), table, table),
+        out_shape=(
+            jax.ShapeDtypeStruct((2 * devs, rows, half), jnp.bfloat16),
+            jax.ShapeDtypeStruct((half, lanes), jnp.bfloat16),
+            jax.ShapeDtypeStruct((half + first.size // lanes, lanes), jnp.bfloat16),
+        ),
         compiler_params=pltpu.CompilerParams(vmem_limit_bytes=SMALL_LIMIT),
         name="partials",
-    )(place, swapped)
-
-
-def merge_kernel(*refs):
-    *part_refs, out_ref = refs
-    depth = part_refs[0].shape[1]
-    for index, ref in enumerate(part_refs):
-        out_ref[:, index * depth : (index + 1) * depth] = ref[...]
-
-
-def merge(*parts):
-    columns, depth = parts[0].shape
-    return pl.pallas_call(
-        merge_kernel,
-        out_shape=jax.ShapeDtypeStruct((columns, depth * len(parts)), jnp.bfloat16),
-        compiler_params=pltpu.CompilerParams(vmem_limit_bytes=SMALL_LIMIT),
-        name="merge",
-    )(*parts)
+    )(flag, swapped, first)
 
 
 def shards(
@@ -269,29 +253,24 @@
         (nx, ny, nz, nc), pair_state, token_pair_mask, alignment_state, alignment_mask, input_weight, alignment_weight
     )
     swap = [(0, 1), (1, 0)]
-    came_a = lax.ppermute(fac_a, "xh", swap)
+    both_a = jnp.concatenate([fac_a, lax.ppermute(fac_a, "c", swap)], 1)
     swapped = lax.all_to_all(send, DEV, split_axis=0, concat_axis=0, tiled=True)
-    both_a = jnp.concatenate([fac_a, came_a], 1)
-    both_a = jnp.concatenate([both_a, lax.ppermute(both_a, "c", swap)], 1)
-    terms = outer_terms(place, both_a, outer_weight, rows)
     state = pair_state.reshape(points, width)
     gate = gates(state, input_weight)
-    swapped, terms, gate = lax.optimization_barrier((swapped, terms, gate))
-    partial, own, away = partials(place, swapped, half)
+    flag = jnp.broadcast_to(jnp.where(lax.axis_index("xh") == 0, 1.0, 0.0), (8, 2 * seqs)).astype(jnp.float32)
+    swapped, both_a, gate, flag = lax.optimization_barrier((swapped, both_a, gate, flag))
+    partial, own, away = partials(flag, swapped, both_a, half)
     back = lax.all_to_all(partial, ("xh",) + DEV, split_axis=0, concat_axis=0, tiled=True)
 
-    table = [
-        own,
-        lax.ppermute(own, "xl", swap),
-        lax.ppermute(away, "xh", swap),
-        lax.ppermute(away, ("xl", "xh"), [(0, 3), (1, 2), (2, 1), (3, 0)]),
-    ]
-    turns = [jnp.concatenate(table, 1)]
-    for turn in range(1, ny):
-        turns.append(lax.ppermute(turns[0], "y", [(i, (i + turn) % ny) for i in range(ny)]))
+    came = lax.ppermute(away, "xh", swap)
+    terms = outer_terms(place, both_a, came[half:], outer_weight, rows)
+    turns = [lax.optimization_barrier(jnp.concatenate([own, came[:half]], 1))]
+    for shift in TURNS[1:]:
+        turns.append(lax.ppermute(turns[0], "y", [(i, (i + shift) % ny) for i in range(ny)]))
+    turns += [lax.ppermute(value, "xl", swap) for value in turns]
     depth = turns[0].shape[1]
-    opm = outer_products(turns[:2], terms)
-    for index in range(2, ny):
+    opm = outer_products(turns[:7], terms)
+    for index in range(7, len(turns)):
         opm = opm + jnp.dot(
             turns[index], terms[index * depth : (index + 1) * depth], preferred_element_type=jnp.float32
         )

time: 80.7 us -> 75.4 us (0.934)
  waiting for transfers between devices: 21.9 us -> 24.9 us
  Pallas kernels: 12.4 us -> 9.61 us
  local copies, waits for them, and re-layouts: 2.63 us -> 0.38 us
  matrix products: 1.85 us -> 0.57 us
  other arithmetic: 3.38 us -> 2.37 us
    all_to_all x1, waiting for transfers between devices: 5.4 us -> 17.2 us  [shards(): swapped = lax.all_to_all(send, DEV, split_axis=0, concat_axis=0, tiled=True)]
    ppermute x8 -> x9, waiting for transfers between devices: 16 us -> 7.13 us  [the longest x3 4.67 us: shards(): lax.ppermute(turns[0], 'y', [(i, (i + shift) % ny) for i in range(ny)])]
    pallas_call x1, Pallas kernels: 4.36 us -> 1.94 us  [outer_terms(): pl.pallas_call(terms_kernel, in_specs=[pl.BlockSpec(memory_space=pltpu.SM...]
    unnamed x15 -> x10, local copies, waits for them, and re-layouts: 2.36 us -> 0.12 us
    all_to_all x1, starting transfers between devices: 8.53 us -> 6.7 us  [shards(): lax.all_to_all(partial, ('xh',) + DEV, split_axis=0, concat_axis=0, tiled...]
    concatenate x2, other arithmetic: 2.07 us -> 0.74 us  [the longest x1 0.72 us: shards(): both_a = jnp.concatenate([fac_a, lax.ppermute(fac_a, 'c', swap)], 1)]
    convert_element_type x0 -> x1, other arithmetic: none -> 0.81 us  [shards(): (state.astype(jnp.float32) + opm + tri_out).astype(jnp.bfloat16)]
    ppermute x8 -> x9, starting transfers between devices: 13.3 us -> 13.7 us  [the longest x4 5.23 us: shards(): turns += [lax.ppermute(value, 'xl', swap) for value in turns]]
  transfers between devices with their start and end apart: 11 -> 12, of which waited for: 6 -> 6; matrix products, arithmetic and copies ran while one was open for 5% -> 3% of each run, Pallas kernels for 9% -> 7%
where the time goes in v3:
time: 75.4 us; the launch traced here: 75.1 us
  starting transfers between devices  37.1 us (49%)
  waiting for transfers between devices  24.9 us (33%)
  Pallas kernels  9.61 us (13%)
  other arithmetic  2.37 us (3%)
    all_to_all x1, waiting for transfers between devices, shards(): swapped = lax.all_to_all(send, DEV, split_axis=0, concat_axis=0, tiled=True)  17.2 us
    all_to_all x1, starting transfers between devices, shards(): swapped = lax.all_to_all(send, DEV, split_axis=0, concat_axis=0, tiled=True)  14.9 us
    all_to_all x1, starting transfers between devices, shards(): lax.all_to_all(partial, ('xh',) + DEV, split_axis=0, concat_axis=0, tiled...  6.7 us
    ppermute x4, starting transfers between devices, shards(): turns += [lax.ppermute(value, 'xl', swap) for value in turns]  5.23 us
    ppermute x3, starting transfers between devices, shards(): lax.ppermute(turns[0], 'y', [(i, (i + shift) % ny) for i in range(ny)])  5.05 us
    ppermute x3, waiting for transfers between devices, shards(): lax.ppermute(turns[0], 'y', [(i, (i + shift) % ny) for i in range(ny)])  4.67 us
    pallas_call x1, Pallas kernels, prepare(): pl.pallas_call(functools.partial(prepare_kernel, grid), out_shape=(jax.Sh...  3.11 us
    ppermute x4, waiting for transfers between devices, shards(): turns += [lax.ppermute(value, 'xl', swap) for value in turns]  2.46 us
  transfers between devices with their start and end apart: 12, of which 6 were waited for; matrix products, arithmetic and copies ran while one was open for 3% of the time, Pallas kernels for 7%

profile of v3, /device:TPU:1, one launch (start us, length us, event | category | flops | bytes accessed | tf_op | source)
XLA Modules:
  0.0 75.1 jit_solution(12187729432577765569)
XLA Ops:
  0.0 0.0 copy-start
  0.0 0.0 copy-start.1
  0.0 3.1 %prepare.1 = (bf16[128,4,640]{2,1,0:T(4,128)(2,1)}, bf16[32,256]{1,0:T(8,128)(2,1)}) custom-call(bf16[4,256,128]{2,1,0:T(8,128)(2,1)} %state_ref.1, s32[4,256]{1,0:T(4,128)} %mask_ref.1, bf16[64,4,64]{2,1,0:T(4,128)(2,1)} %align_ref.1, s32[4,64]{1,0:T(4,128)} %bitcast.29, bf16[128,640]{1,0:T(8,128)(2,1)} %weight_ref.4, bf16[64,64]{1,0:T(8,128)(2,1)} %align_weight_ref.1), custom_call_target="tpu_custom_call" | custom-call | tf_op jit(solution)/shard_map/prepare/pallas_call | solution.py:77
  3.1 14.9 %all-to-all-start = ((bf16[128,4,640]{2,1,0:T(4,128)(2,1)}), bf16[128,4,640]{2,1,0:T(4,128)(2,1)S(1)}, u32[]{:S(2)}, u32[]{:S(2)}) async-start(bf16[128,4,640]{2,1,0:T(4,128)(2,1)} %get-tuple-element.16), calls=%async_computation | async-start | bytes 1310720 | tf_op jit(solution)/shard_map/all_to_all | solution.py:257
  18.0 1.0 %collective-permute-start = (bf16[32,256]{1,0:T(8,128)(2,1)}, bf16[32,256]{1,0:T(8,128)(2,1)S(1)}, u32[]{:S(2)}, u32[]{:S(2)}) collective-permute-start(bf16[32,256]{1,0:T(8,128)(2,1)} %get-tuple-element.17), channel_id=1, source_target_pairs={{0,2},{2,0},{1,3},{3,1},{4,6},{6,4},{5,7},{7,5},{8,10},{10,8},{9,1... | collective-permute-start | bytes 49160 | tf_op jit(solution)/shard_map/ppermute | solution.py:256
  19.0 2.3 %gates.1 = f32[1024,128]{1,0:T(8,128)} custom-call(bf16[1024,128]{1,0:T(8,128)(2,1)} %bitcast.24, bf16[128,640]{1,0:T(8,128)(2,1)} %weight_ref.4), custom_call_target="tpu_custom_call" | custom-call | tf_op jit(solution)/shard_map/gates/pallas_call | solution.py:99
  21.2 0.0 collective-permute-done
  21.2 0.7 pad_maximum_fusion.1.first_ref
  22.0 17.2 %all-to-all-done.swapped_ref = bf16[128,4,640]{2,1,0:T(4,128)(2,1)S(1)} async-done(((bf16[128,4,640]{2,1,0:T(4,128)(2,1)}), bf16[128,4,640]{2,1,0:T(4,128)(2,1)S(1)}, u32[]{:S(2)}, u32[]{:S(2)}) %all-to-all-start) | async-done | bytes 655392 | tf_op jit(solution)/shard_map/all_to_all | solution.py:257
  39.2 1.2 %partials.1 = (bf16[256,4,256]{2,1,0:T(4,128)(2,1)}, bf16[256,128]{1,0:T(8,128)(2,1)S(1)}, bf16[384,128]{1,0:T(8,128)(2,1)S(1)}) custom-call(f32[8,128]{1,0:T(8,128)S(1)} %broadcast_in_dim.2.flag_ref, bf16[128,4,640]{2,1,0:T(4,128)(2,1)S(1)} %all-to-all-done.swapped_ref, bf16[32,512]{1,0:T(8,128)(2,1)S(1)} %pad_maximum_fusion.1.first_ref), custom_call_target="tpu_custom_call" | custom-call | tf_op jit(solution)/shard_map/partials/pallas_call | solution.py:222
  40.4 2.5 %collective-permute-start.1 = (bf16[384,128]{1,0:T(8,128)(2,1)S(1)}, bf16[384,128]{1,0:T(8,128)(2,1)S(1)}, u32[]{:S(2)}, u32[]{:S(2)}) collective-permute-start(bf16[384,128]{1,0:T(8,128)(2,1)S(1)} %get-tuple-element.22), channel_id=1, source_target_pairs={{0,1},{1,0},{2,3},{3,2},{4,5},{5,4},{6,7},{7,6},{8,9},{9,8},{10,11... | collective-permute-start | bytes 294920 | tf_op jit(solution)/shard_map/ppermute | solution.py:265
  42.8 6.7 %all-to-all-start.1 = ((bf16[256,4,256]{2,1,0:T(4,128)(2,1)}), bf16[256,4,256]{2,1,0:T(4,128)(2,1)S(1)}, u32[]{:S(2)}, u32[]{:S(2)}) async-start(bf16[256,4,256]{2,1,0:T(4,128)(2,1)} %get-tuple-element.23), calls=%async_computation.1 | async-start | bytes 1048576 | tf_op jit(solution)/shard_map/all_to_all | solution.py:263
  49.5 0.0 collective-permute-done.1
  49.6 1.5 %collective-permute-start.3 = (bf16[256,256]{1,0:T(8,128)(2,1)S(1)}, bf16[256,256]{1,0:T(8,128)(2,1)S(1)}, u32[]{:S(2)}, u32[]{:S(2)}) collective-permute-start(bf16[256,256]{1,0:T(8,128)(2,1)S(1)} %pad_maximum_fusion.refs_0_), channel_id=1, source_target_pairs={{0,32},{32,64},{64,96},{96,0},{1,33},{33,65},{65,97},{97,1},{2,34}... | collective-permute-start | bytes 393224 | tf_op jit(solution)/shard_map/ppermute | solution.py:269
  51.0 2.4 %collective-permute-start.2 = (bf16[256,256]{1,0:T(8,128)(2,1)S(1)}, bf16[256,256]{1,0:T(8,128)(2,1)S(1)}, u32[]{:S(2)}, u32[]{:S(2)}) collective-permute-start(bf16[256,256]{1,0:T(8,128)(2,1)S(1)} %pad_maximum_fusion.refs_0_), channel_id=1, source_target_pairs={{0,64},{32,96},{64,0},{96,32},{1,65},{33,97},{65,1},{97,33},{2,66}... | collective-permute-start | bytes 393224 | tf_op jit(solution)/shard_map/ppermute | solution.py:269
  53.5 1.1 %collective-permute-start.4 = (bf16[256,256]{1,0:T(8,128)(2,1)S(1)}, bf16[256,256]{1,0:T(8,128)(2,1)S(1)}, u32[]{:S(2)}, u32[]{:S(2)}) collective-permute-start(bf16[256,256]{1,0:T(8,128)(2,1)S(1)} %pad_maximum_fusion.refs_0_), channel_id=1, source_target_pairs={{0,96},{32,0},{64,32},{96,64},{1,97},{33,1},{65,33},{97,65},{2,98}... | collective-permute-start | bytes 393224 | tf_op jit(solution)/shard_map/ppermute | solution.py:269
  54.6 1.2 %collective-permute-start.5 = (bf16[256,256]{1,0:T(8,128)(2,1)S(1)}, bf16[256,256]{1,0:T(8,128)(2,1)S(1)}, u32[]{:S(2)}, u32[]{:S(2)}) collective-permute-start(bf16[256,256]{1,0:T(8,128)(2,1)S(1)} %pad_maximum_fusion.refs_0_), channel_id=1, source_target_pairs={{0,128},{128,0},{1,129},{129,1},{2,130},{130,2},{3,131},{131,3},{4... | collective-permute-start | bytes 393224 | tf_op jit(solution)/shard_map/ppermute | solution.py:270
  55.8 0.0 collective-permute-done.3.refs_2_
  55.8 2.3 %collective-permute-start.7 = (bf16[256,256]{1,0:T(8,128)(2,1)S(1)}, bf16[256,256]{1,0:T(8,128)(2,1)S(1)}, u32[]{:S(2)}, u32[]{:S(2)}) collective-permute-start(bf16[256,256]{1,0:T(8,128)(2,1)S(1)} %collective-permute-done.3.refs_2_), channel_id=1, source_target_pairs={{0,128},{128,0},{1,129},{129,1},{2,130},{130,2},{3,131},{131,3},{4... | collective-permute-start | bytes 393224 | tf_op jit(solution)/shard_map/ppermute | solution.py:270
  58.1 4.7 %collective-permute-done.2.refs_1_ = bf16[256,256]{1,0:T(8,128)(2,1)S(1)} collective-permute-done((bf16[256,256]{1,0:T(8,128)(2,1)S(1)}, bf16[256,256]{1,0:T(8,128)(2,1)S(1)}, u32[]{:S(2)}, u32[]{:S(2)}) %collective-permute-start.2) | collective-permute-done | bytes 131104 | tf_op jit(solution)/shard_map/ppermute | solution.py:269
  62.8 1.7 %collective-permute-start.6 = (bf16[256,256]{1,0:T(8,128)(2,1)S(1)}, bf16[256,256]{1,0:T(8,128)(2,1)S(1)}, u32[]{:S(2)}, u32[]{:S(2)}) collective-permute-start(bf16[256,256]{1,0:T(8,128)(2,1)S(1)} %collective-permute-done.2.refs_1_), channel_id=1, source_target_pairs={{0,128},{128,0},{1,129},{129,1},{2,130},{130,2},{3,131},{131,3},{4... | collective-permute-start | bytes 393224 | tf_op jit(solution)/shard_map/ppermute | solution.py:270
  64.5 0.0 collective-permute-done.4.refs_3_
  64.5 0.0 collective-permute-start.8
  64.5 0.1 pad_add_fusion.place_ref
  64.6 0.0 copy-done.1
  64.6 1.9 %outer_terms.1.refs_7_ = bf16[2048,1024]{1,0:T(8,128)(2,1)S(1)} custom-call(s32[4]{0:T(128)S(1)} %pad_add_fusion.place_ref, bf16[32,512]{1,0:T(8,128)(2,1)S(1)} %pad_maximum_fusion.1.first_ref, bf16[128,128]{1,0:T(8,128)(2,1)S(1)} %slice.32.came_ref, bf16[1024,128]{1,0:T(8,128)(2,1)S(1)} %copy-done.1), custom_call_target="tpu_custom_call" | custom-call | flops 134217728 | bytes 4194304 | tf_op jit(solution)/shard_map/outer_terms/pallas_call | solution.py:146
  66.6 0.0 collective-permute-done.5.refs_4_
  66.6 0.0 collective-permute-done.7.refs_6_
  66.6 1.0 %collective-permute-done.6.refs_5_ = bf16[256,256]{1,0:T(8,128)(2,1)S(1)} collective-permute-done((bf16[256,256]{1,0:T(8,128)(2,1)S(1)}, bf16[256,256]{1,0:T(8,128)(2,1)S(1)}, u32[]{:S(2)}, u32[]{:S(2)}) %collective-permute-start.6) | collective-permute-done | bytes 131104 | tf_op jit(solution)/shard_map/ppermute | solution.py:270
  67.5 1.1 %outer_products.1 = f32[256,1024]{1,0:T(8,128)S(1)} custom-call(bf16[256,256]{1,0:T(8,128)(2,1)S(1)} %pad_maximum_fusion.refs_0_, bf16[256,256]{1,0:T(8,128)(2,1)S(1)} %collective-permute-done.2.refs_1_, bf16[256,256]{1,0:T(8,128)(2,1)S(1)} %collective-permute-done.3.refs_2_, bf16[256,256]{1,0:T(8,128)(2,1)S(1)} %collective-permute-done.4.refs_3_, ...), custom_call_target="tpu_custom_call" | custom-call | flops 939524096 | bytes 5636096 | tf_op jit(solution)/shard_map/outer_products/pallas_call | solution.py:173
  68.6 1.5 %collective-permute-done.8 = bf16[256,256]{1,0:T(8,128)(2,1)S(1)} collective-permute-done((bf16[256,256]{1,0:T(8,128)(2,1)S(1)}, bf16[256,256]{1,0:T(8,128)(2,1)S(1)}, u32[]{:S(2)}, u32[]{:S(2)}) %collective-permute-start.8) | collective-permute-done | bytes 131104 | tf_op jit(solution)/shard_map/ppermute | solution.py:270
  70.1 0.3 fusion.1
  70.4 0.2 add_multiply_fusion
  70.7 0.3 all-to-all-done.1
  71.0 1.8 %collective-permute-start.9 = (bf16[256,512]{1,0:T(8,128)(2,1)S(1)}, bf16[256,512]{1,0:T(8,128)(2,1)S(1)}, u32[]{:S(2)}, u32[]{:S(2)}) collective-permute-start(bf16[256,512]{1,0:T(8,128)(2,1)S(1)} %slice.50), channel_id=1, source_target_pairs={{0,2},{2,0},{1,3},{3,1},{4,6},{6,4},{5,7},{7,5},{8,10},{10,8},{9,1... | collective-permute-start | bytes 786440 | tf_op jit(solution)/shard_map/ppermute | solution.py:280
  72.8 0.1 convert_element_type.31
  72.9 0.0 copy-start.2
  72.9 0.0 copy-start.3
  72.9 0.3 fusion.9
  73.2 0.1 copy.10
  73.3 0.1 multiply_reduce_fusion
  73.4 0.0 copy-done
  73.4 0.3 fusion.5
  73.7 0.2 collective-permute-done.9
  73.9 0.1 slice_add_fusion.1
  74.0 0.2 reshape.38
  74.2 0.0 copy-done.2
  74.2 0.0 copy-done.3
  74.3 0.8 %fusion.4 = bf16[1024,128]{1,0:T(8,128)(2,1)} fusion(f32[4,256,128]{2,1,0:T(8,128)S(1)} %copy.9, f32[1024,128]{1,0:T(8,128)S(1)} %copy-done.3, f32[1024,128]{1,0:T(8,128)S(1)} %fusion.5, bf16[4,256,128]{2,1,0:T(8,128)(2,1)S(1)} %copy-done.2), kind=kLoop, calls=%fused_computation.9 | loop fusion | flops 655360 | bytes 2097152 | tf_op jit(solution)/shard_map/convert_element_type | solution.py:290
  (9 shorter events, 0.1 us)
Async XLA Ops:
  0.0 73.4 %copy-start = (bf16[128,128]{1,0:T(8,128)(2,1)S(1)}, bf16[128,128]{1,0:T(8,128)(2,1)}, u32[]{:S(2)}) copy-start(bf16[128,128]{1,0:T(8,128)(2,1)} %param.13) | copy-start | bytes 98308
  0.0 64.6 %copy-start.1 = (bf16[1024,128]{1,0:T(8,128)(2,1)S(1)}, bf16[1024,128]{1,0:T(8,128)(2,1)}, u32[]{:S(2)}) copy-start(bf16[1024,128]{1,0:T(8,128)(2,1)} %weight_ref.5) | copy-start | bytes 786436
  3.1 36.1 %all-to-all-start = ((bf16[128,4,640]{2,1,0:T(4,128)(2,1)}), bf16[128,4,640]{2,1,0:T(4,128)(2,1)S(1)}, u32[]{:S(2)}, u32[]{:S(2)}) async-start(bf16[128,4,640]{2,1,0:T(4,128)(2,1)} %get-tuple-element.16), calls=%async_computation | async-start | bytes 1310720 | tf_op jit(solution)/shard_map/all_to_all | solution.py:257
  18.0 3.3 %collective-permute-start = (bf16[32,256]{1,0:T(8,128)(2,1)}, bf16[32,256]{1,0:T(8,128)(2,1)S(1)}, u32[]{:S(2)}, u32[]{:S(2)}) collective-permute-start(bf16[32,256]{1,0:T(8,128)(2,1)} %get-tuple-element.17), channel_id=1, source_target_pairs={{0,2},{2,0},{1,3},{3,1},{4,6},{6,4},{5,7},{7,5},{8,10},{10,8},{9,1... | collective-permute-start | bytes 49160 | tf_op jit(solution)/shard_map/ppermute | solution.py:256
  40.4 9.2 %collective-permute-start.1 = (bf16[384,128]{1,0:T(8,128)(2,1)S(1)}, bf16[384,128]{1,0:T(8,128)(2,1)S(1)}, u32[]{:S(2)}, u32[]{:S(2)}) collective-permute-start(bf16[384,128]{1,0:T(8,128)(2,1)S(1)} %get-tuple-element.22), channel_id=1, source_target_pairs={{0,1},{1,0},{2,3},{3,2},{4,5},{5,4},{6,7},{7,6},{8,9},{9,8},{10,11... | collective-permute-start | bytes 294920 | tf_op jit(solution)/shard_map/ppermute | solution.py:265
  42.8 28.1 %all-to-all-start.1 = ((bf16[256,4,256]{2,1,0:T(4,128)(2,1)}), bf16[256,4,256]{2,1,0:T(4,128)(2,1)S(1)}, u32[]{:S(2)}, u32[]{:S(2)}) async-start(bf16[256,4,256]{2,1,0:T(4,128)(2,1)} %get-tuple-element.23), calls=%async_computation.1 | async-start | bytes 1048576 | tf_op jit(solution)/shard_map/all_to_all | solution.py:263
  49.6 6.2 %collective-permute-start.3 = (bf16[256,256]{1,0:T(8,128)(2,1)S(1)}, bf16[256,256]{1,0:T(8,128)(2,1)S(1)}, u32[]{:S(2)}, u32[]{:S(2)}) collective-permute-start(bf16[256,256]{1,0:T(8,128)(2,1)S(1)} %pad_maximum_fusion.refs_0_), channel_id=1, source_target_pairs={{0,32},{32,64},{64,96},{96,0},{1,33},{33,65},{65,97},{97,1},{2,34}... | collective-permute-start | bytes 393224 | tf_op jit(solution)/shard_map/ppermute | solution.py:269
  51.0 11.7 %collective-permute-start.2 = (bf16[256,256]{1,0:T(8,128)(2,1)S(1)}, bf16[256,256]{1,0:T(8,128)(2,1)S(1)}, u32[]{:S(2)}, u32[]{:S(2)}) collective-permute-start(bf16[256,256]{1,0:T(8,128)(2,1)S(1)} %pad_maximum_fusion.refs_0_), channel_id=1, source_target_pairs={{0,64},{32,96},{64,0},{96,32},{1,65},{33,97},{65,1},{97,33},{2,66}... | collective-permute-start | bytes 393224 | tf_op jit(solution)/shard_map/ppermute | solution.py:269
  53.5 11.0 %collective-permute-start.4 = (bf16[256,256]{1,0:T(8,128)(2,1)S(1)}, bf16[256,256]{1,0:T(8,128)(2,1)S(1)}, u32[]{:S(2)}, u32[]{:S(2)}) collective-permute-start(bf16[256,256]{1,0:T(8,128)(2,1)S(1)} %pad_maximum_fusion.refs_0_), channel_id=1, source_target_pairs={{0,96},{32,0},{64,32},{96,64},{1,97},{33,1},{65,33},{97,65},{2,98}... | collective-permute-start | bytes 393224 | tf_op jit(solution)/shard_map/ppermute | solution.py:269
  54.6 11.9 %collective-permute-start.5 = (bf16[256,256]{1,0:T(8,128)(2,1)S(1)}, bf16[256,256]{1,0:T(8,128)(2,1)S(1)}, u32[]{:S(2)}, u32[]{:S(2)}) collective-permute-start(bf16[256,256]{1,0:T(8,128)(2,1)S(1)} %pad_maximum_fusion.refs_0_), channel_id=1, source_target_pairs={{0,128},{128,0},{1,129},{129,1},{2,130},{130,2},{3,131},{131,3},{4... | collective-permute-start | bytes 393224 | tf_op jit(solution)/shard_map/ppermute | solution.py:270
  55.8 10.8 %collective-permute-start.7 = (bf16[256,256]{1,0:T(8,128)(2,1)S(1)}, bf16[256,256]{1,0:T(8,128)(2,1)S(1)}, u32[]{:S(2)}, u32[]{:S(2)}) collective-permute-start(bf16[256,256]{1,0:T(8,128)(2,1)S(1)} %collective-permute-done.3.refs_2_), channel_id=1, source_target_pairs={{0,128},{128,0},{1,129},{129,1},{2,130},{130,2},{3,131},{131,3},{4... | collective-permute-start | bytes 393224 | tf_op jit(solution)/shard_map/ppermute | solution.py:270
  62.8 4.7 %collective-permute-start.6 = (bf16[256,256]{1,0:T(8,128)(2,1)S(1)}, bf16[256,256]{1,0:T(8,128)(2,1)S(1)}, u32[]{:S(2)}, u32[]{:S(2)}) collective-permute-start(bf16[256,256]{1,0:T(8,128)(2,1)S(1)} %collective-permute-done.2.refs_1_), channel_id=1, source_target_pairs={{0,128},{128,0},{1,129},{129,1},{2,130},{130,2},{3,131},{131,3},{4... | collective-permute-start | bytes 393224 | tf_op jit(solution)/shard_map/ppermute | solution.py:270
  64.5 5.6 %collective-permute-start.8 = (bf16[256,256]{1,0:T(8,128)(2,1)S(1)}, bf16[256,256]{1,0:T(8,128)(2,1)S(1)}, u32[]{:S(2)}, u32[]{:S(2)}) collective-permute-start(bf16[256,256]{1,0:T(8,128)(2,1)S(1)} %collective-permute-done.4.refs_3_), channel_id=1, source_target_pairs={{0,128},{128,0},{1,129},{129,1},{2,130},{130,2},{3,131},{131,3},{4... | collective-permute-start | bytes 393224 | tf_op jit(solution)/shard_map/ppermute | solution.py:270
  71.0 3.0 %collective-permute-start.9 = (bf16[256,512]{1,0:T(8,128)(2,1)S(1)}, bf16[256,512]{1,0:T(8,128)(2,1)S(1)}, u32[]{:S(2)}, u32[]{:S(2)}) collective-permute-start(bf16[256,512]{1,0:T(8,128)(2,1)S(1)} %slice.50), channel_id=1, source_target_pairs={{0,2},{2,0},{1,3},{3,1},{4,6},{6,4},{5,7},{7,5},{8,10},{10,8},{9,1... | collective-permute-start | bytes 786440 | tf_op jit(solution)/shard_map/ppermute | solution.py:280
  72.9 1.3 %copy-start.2 = (bf16[4,256,128]{2,1,0:T(8,128)(2,1)S(1)}, bf16[4,256,128]{2,1,0:T(8,128)(2,1)}, u32[]{:S(2)}) copy-start(bf16[4,256,128]{2,1,0:T(8,128)(2,1)} %state_ref.1) | copy-start | bytes 786436
  72.9 1.3 %copy-start.3 = (f32[1024,128]{1,0:T(8,128)S(1)}, f32[1024,128]{1,0:T(8,128)}, u32[]{:S(2)}) copy-start(f32[1024,128]{1,0:T(8,128)} %gates.1) | copy-start | bytes 1572868

commit v4 on v3

--- a/solution.py
+++ b/solution.py
@@ -155,7 +155,7 @@
     )(place, first, came, weight)
 
 
-def outer_kernel(*refs):
+def early_kernel(*refs):
     *turn_refs, terms_ref, out_ref = refs
     depth = turn_refs[0].shape[1]
     total = 0.0
@@ -166,12 +166,12 @@
     out_ref[...] = total
 
 
-def outer_products(turns, terms):
+def early_products(turns, terms):
     columns, depth = turns[0].shape
     width = terms.shape[1]
     count = len(turns)
     return pl.pallas_call(
-        outer_kernel,
+        early_kernel,
         out_shape=jax.ShapeDtypeStruct((columns, width), jnp.float32),
         cost_estimate=pl.CostEstimate(
             flops=2 * columns * depth * count * width,
@@ -179,8 +179,43 @@
             transcendentals=0,
         ),
         compiler_params=pltpu.CompilerParams(vmem_limit_bytes=SMALL_LIMIT),
-        name="outer_products",
+        name="early_products",
     )(*turns, terms)
+
+
+def late_kernel(offset, *refs):
+    *turn_refs, total_ref, terms_ref, own_ref, other_ref = refs
+    depth = turn_refs[0].shape[1]
+    rows, _, width = own_ref.shape
+    total = total_ref[...]
+    for index, ref in enumerate(turn_refs):
+        start = offset + index * depth
+        total = total + jnp.dot(ref[...], terms_ref[start : start + depth, :], preferred_element_type=jnp.float32)
+    total = total * (1.0 / ALIGNMENT_ROWS)
+    for row in range(rows):
+        own_ref[row] = total[:, row * width : (row + 1) * width]
+        other_ref[row] = total[:, (rows + row) * width : (rows + row + 1) * width].astype(jnp.bfloat16)
+
+
+def late_products(turns, total, terms, rows):
+    columns, depth = turns[0].shape
+    width = terms.shape[1]
+    shape = (rows, columns, width // 2 // rows)
+    count = len(turns)
+    return pl.pallas_call(
+        functools.partial(late_kernel, terms.shape[0] - count * depth),
+        out_shape=(
+            jax.ShapeDtypeStruct(shape, jnp.float32),
+            jax.ShapeDtypeStruct(shape, jnp.bfloat16),
+        ),
+        cost_estimate=pl.CostEstimate(
+            flops=2 * columns * depth * count * width,
+            bytes_accessed=2 * depth * count * (width + columns) + 7 * columns * width,
+            transcendentals=0,
+        ),
+        compiler_params=pltpu.CompilerParams(vmem_limit_bytes=SMALL_LIMIT),
+        name="late_products",
+    )(*turns, total, terms)
 
 
 def compact(values):
@@ -269,13 +304,12 @@
         turns.append(lax.ppermute(turns[0], "y", [(i, (i + shift) % ny) for i in range(ny)]))
     turns += [lax.ppermute(value, "xl", swap) for value in turns]
     depth = turns[0].shape[1]
-    opm = outer_products(turns[:7], terms)
-    for index in range(7, len(turns)):
+    opm = early_products(turns[:5], terms)
+    for index in range(5, 7):
         opm = opm + jnp.dot(
             turns[index], terms[index * depth : (index + 1) * depth], preferred_element_type=jnp.float32
         )
-    opm = opm * (1.0 / ALIGNMENT_ROWS)
-    opm, other = opm[:, : rows * width], opm[:, rows * width :].astype(jnp.bfloat16)
+    opm, other = late_products(turns[7:], opm, terms, rows)
     other, back = lax.optimization_barrier((other, back))
     other = lax.ppermute(other, "c", swap)
 
@@ -285,9 +319,8 @@
     tri_out = gate * jnp.einsum(
         "cp,cd->pd", tri_norm, output_weight, preferred_element_type=jnp.float32
     )
-    opm = (opm + other.astype(jnp.float32)).reshape(half, rows, width)
-    opm = jnp.transpose(opm, (1, 0, 2)).reshape(points, width)
-    return (state.astype(jnp.float32) + opm + tri_out).astype(jnp.bfloat16).reshape(rows, half, width)
+    base = lax.optimization_barrier(state.astype(jnp.float32) + tri_out + opm.reshape(points, width))
+    return (base + other.reshape(points, width).astype(jnp.float32)).astype(jnp.bfloat16).reshape(rows, half, width)
 
 
 def solution(mesh):

time: 75.4 us -> 74.8 us (level)
    ppermute x3, waiting for transfers between devices: 4.67 us -> 2.64 us  [shards(): lax.ppermute(turns[0], 'y', [(i, (i + shift) % ny) for i in range(ny)])]
    ppermute x4, waiting for transfers between devices: 2.46 us -> 4.15 us  [shards(): turns += [lax.ppermute(value, 'xl', swap) for value in turns]]
where the time goes in v4:
time: 74.8 us; the launch traced here: 74.5 us
  starting transfers between devices  36.9 us (49%)
  waiting for transfers between devices  24.6 us (33%)
  Pallas kernels  9.67 us (13%)
  other arithmetic  2.19 us (3%)
  matrix products  0.87 us (1%)
    all_to_all x1, waiting for transfers between devices, shards(): swapped = lax.all_to_all(send, DEV, split_axis=0, concat_axis=0, tiled=True)  17.2 us
    all_to_all x1, starting transfers between devices, shards(): swapped = lax.all_to_all(send, DEV, split_axis=0, concat_axis=0, tiled=True)  14.9 us
    all_to_all x1, starting transfers between devices, shards(): lax.all_to_all(partial, ('xh',) + DEV, split_axis=0, concat_axis=0, tiled...  6.7 us
    ppermute x4, starting transfers between devices, shards(): turns += [lax.ppermute(value, 'xl', swap) for value in turns]  5.23 us
    ppermute x3, starting transfers between devices, shards(): lax.ppermute(turns[0], 'y', [(i, (i + shift) % ny) for i in range(ny)])  5.05 us
    ppermute x4, waiting for transfers between devices, shards(): turns += [lax.ppermute(value, 'xl', swap) for value in turns]  4.15 us
    pallas_call x1, Pallas kernels, prepare(): pl.pallas_call(functools.partial(prepare_kernel, grid), out_shape=(jax.Sh...  3.11 us
    ppermute x3, waiting for transfers between devices, shards(): lax.ppermute(turns[0], 'y', [(i, (i + shift) % ny) for i in range(ny)])  2.64 us
  transfers between devices with their start and end apart: 12, of which 6 were waited for; matrix products, arithmetic and copies ran while one was open for 3% of the time, Pallas kernels for 7%

profile of v4, /device:TPU:1, one launch (start us, length us, event | category | flops | bytes accessed | tf_op | source)
XLA Modules:
  0.0 74.5 jit_solution(11510540629359992905)
XLA Ops:
  0.0 0.0 copy-start
  0.0 0.0 copy-start.1
  0.0 3.1 %prepare.1 = (bf16[128,4,640]{2,1,0:T(4,128)(2,1)}, bf16[32,256]{1,0:T(8,128)(2,1)}) custom-call(bf16[4,256,128]{2,1,0:T(8,128)(2,1)} %state_ref.1, s32[4,256]{1,0:T(4,128)} %mask_ref.1, bf16[64,4,64]{2,1,0:T(4,128)(2,1)} %align_ref.1, s32[4,64]{1,0:T(4,128)} %bitcast.27, bf16[128,640]{1,0:T(8,128)(2,1)} %weight_ref.4, bf16[64,64]{1,0:T(8,128)(2,1)} %align_weight_ref.1), custom_call_target="tpu_custom_call" | custom-call | tf_op jit(solution)/shard_map/prepare/pallas_call | solution.py:77
  3.1 14.9 %all-to-all-start = ((bf16[128,4,640]{2,1,0:T(4,128)(2,1)}), bf16[128,4,640]{2,1,0:T(4,128)(2,1)S(1)}, u32[]{:S(2)}, u32[]{:S(2)}) async-start(bf16[128,4,640]{2,1,0:T(4,128)(2,1)} %get-tuple-element.18), calls=%async_computation | async-start | bytes 1310720 | tf_op jit(solution)/shard_map/all_to_all | solution.py:292
  18.0 1.0 %collective-permute-start = (bf16[32,256]{1,0:T(8,128)(2,1)}, bf16[32,256]{1,0:T(8,128)(2,1)S(1)}, u32[]{:S(2)}, u32[]{:S(2)}) collective-permute-start(bf16[32,256]{1,0:T(8,128)(2,1)} %get-tuple-element.19), channel_id=1, source_target_pairs={{0,2},{2,0},{1,3},{3,1},{4,6},{6,4},{5,7},{7,5},{8,10},{10,8},{9,1... | collective-permute-start | bytes 49160 | tf_op jit(solution)/shard_map/ppermute | solution.py:291
  19.0 2.3 %gates.1 = f32[1024,128]{1,0:T(8,128)} custom-call(bf16[1024,128]{1,0:T(8,128)(2,1)} %bitcast.23, bf16[128,640]{1,0:T(8,128)(2,1)} %weight_ref.4), custom_call_target="tpu_custom_call" | custom-call | tf_op jit(solution)/shard_map/gates/pallas_call | solution.py:99
  21.3 0.0 collective-permute-done
  21.3 0.7 pad_maximum_fusion.1.first_ref
  22.0 17.2 %all-to-all-done.swapped_ref = bf16[128,4,640]{2,1,0:T(4,128)(2,1)S(1)} async-done(((bf16[128,4,640]{2,1,0:T(4,128)(2,1)}), bf16[128,4,640]{2,1,0:T(4,128)(2,1)S(1)}, u32[]{:S(2)}, u32[]{:S(2)}) %all-to-all-start) | async-done | bytes 655392 | tf_op jit(solution)/shard_map/all_to_all | solution.py:292
  39.2 1.2 %partials.1 = (bf16[256,4,256]{2,1,0:T(4,128)(2,1)}, bf16[256,128]{1,0:T(8,128)(2,1)S(1)}, bf16[384,128]{1,0:T(8,128)(2,1)S(1)}) custom-call(f32[8,128]{1,0:T(8,128)S(1)} %broadcast_in_dim.2.flag_ref, bf16[128,4,640]{2,1,0:T(4,128)(2,1)S(1)} %all-to-all-done.swapped_ref, bf16[32,512]{1,0:T(8,128)(2,1)S(1)} %pad_maximum_fusion.1.first_ref), custom_call_target="tpu_custom_call" | custom-call | tf_op jit(solution)/shard_map/partials/pallas_call | solution.py:257
  40.4 2.4 %collective-permute-start.1 = (bf16[384,128]{1,0:T(8,128)(2,1)S(1)}, bf16[384,128]{1,0:T(8,128)(2,1)S(1)}, u32[]{:S(2)}, u32[]{:S(2)}) collective-permute-start(bf16[384,128]{1,0:T(8,128)(2,1)S(1)} %get-tuple-element.25), channel_id=1, source_target_pairs={{0,1},{1,0},{2,3},{3,2},{4,5},{5,4},{6,7},{7,6},{8,9},{9,8},{10,11... | collective-permute-start | bytes 294920 | tf_op jit(solution)/shard_map/ppermute | solution.py:300
  42.8 6.7 %all-to-all-start.1 = ((bf16[256,4,256]{2,1,0:T(4,128)(2,1)}), bf16[256,4,256]{2,1,0:T(4,128)(2,1)S(1)}, u32[]{:S(2)}, u32[]{:S(2)}) async-start(bf16[256,4,256]{2,1,0:T(4,128)(2,1)} %get-tuple-element.27), calls=%async_computation.1 | async-start | bytes 1048576 | tf_op jit(solution)/shard_map/all_to_all | solution.py:298
  49.5 0.0 collective-permute-done.1
  49.6 1.5 %collective-permute-start.5 = (bf16[256,256]{1,0:T(8,128)(2,1)S(1)}, bf16[256,256]{1,0:T(8,128)(2,1)S(1)}, u32[]{:S(2)}, u32[]{:S(2)}) collective-permute-start(bf16[256,256]{1,0:T(8,128)(2,1)S(1)} %pad_maximum_fusion.refs_0_), channel_id=1, source_target_pairs={{0,32},{32,64},{64,96},{96,0},{1,33},{33,65},{65,97},{97,1},{2,34}... | collective-permute-start | bytes 393224 | tf_op jit(solution)/shard_map/ppermute | solution.py:304
  51.1 2.4 %collective-permute-start.4 = (bf16[256,256]{1,0:T(8,128)(2,1)S(1)}, bf16[256,256]{1,0:T(8,128)(2,1)S(1)}, u32[]{:S(2)}, u32[]{:S(2)}) collective-permute-start(bf16[256,256]{1,0:T(8,128)(2,1)S(1)} %pad_maximum_fusion.refs_0_), channel_id=1, source_target_pairs={{0,64},{32,96},{64,0},{96,32},{1,65},{33,97},{65,1},{97,33},{2,66}... | collective-permute-start | bytes 393224 | tf_op jit(solution)/shard_map/ppermute | solution.py:304
  53.5 1.1 %collective-permute-start.2 = (bf16[256,256]{1,0:T(8,128)(2,1)S(1)}, bf16[256,256]{1,0:T(8,128)(2,1)S(1)}, u32[]{:S(2)}, u32[]{:S(2)}) collective-permute-start(bf16[256,256]{1,0:T(8,128)(2,1)S(1)} %pad_maximum_fusion.refs_0_), channel_id=1, source_target_pairs={{0,96},{32,0},{64,32},{96,64},{1,97},{33,1},{65,33},{97,65},{2,98}... | collective-permute-start | bytes 393224 | tf_op jit(solution)/shard_map/ppermute | solution.py:304
  54.6 1.2 %collective-permute-start.6 = (bf16[256,256]{1,0:T(8,128)(2,1)S(1)}, bf16[256,256]{1,0:T(8,128)(2,1)S(1)}, u32[]{:S(2)}, u32[]{:S(2)}) collective-permute-start(bf16[256,256]{1,0:T(8,128)(2,1)S(1)} %pad_maximum_fusion.refs_0_), channel_id=1, source_target_pairs={{0,128},{128,0},{1,129},{129,1},{2,130},{130,2},{3,131},{131,3},{4... | collective-permute-start | bytes 393224 | tf_op jit(solution)/shard_map/ppermute | solution.py:305
  55.8 0.0 collective-permute-done.5.refs_2_
  55.8 2.3 %collective-permute-start.8 = (bf16[256,256]{1,0:T(8,128)(2,1)S(1)}, bf16[256,256]{1,0:T(8,128)(2,1)S(1)}, u32[]{:S(2)}, u32[]{:S(2)}) collective-permute-start(bf16[256,256]{1,0:T(8,128)(2,1)S(1)} %collective-permute-done.5.refs_2_), channel_id=1, source_target_pairs={{0,128},{128,0},{1,129},{129,1},{2,130},{130,2},{3,131},{131,3},{4... | collective-permute-start | bytes 393224 | tf_op jit(solution)/shard_map/ppermute | solution.py:305
  58.1 0.1 pad_add_fusion.place_ref
  58.2 0.0 copy-done.1
  58.2 1.9 %outer_terms.1.refs_5_.refs_2_ = bf16[2048,1024]{1,0:T(8,128)(2,1)S(1)} custom-call(s32[4]{0:T(128)S(1)} %pad_add_fusion.place_ref, bf16[32,512]{1,0:T(8,128)(2,1)S(1)} %pad_maximum_fusion.1.first_ref, bf16[128,128]{1,0:T(8,128)(2,1)S(1)} %slice.27.came_ref, bf16[1024,128]{1,0:T(8,128)(2,1)S(1)} %copy-done.1), custom_call_target="tpu_custom_call" | custom-call | flops 134217728 | bytes 4194304 | tf_op jit(solution)/shard_map/outer_terms/pallas_call | solution.py:146
  60.2 2.6 %collective-permute-done.4.refs_1_ = bf16[256,256]{1,0:T(8,128)(2,1)S(1)} collective-permute-done((bf16[256,256]{1,0:T(8,128)(2,1)S(1)}, bf16[256,256]{1,0:T(8,128)(2,1)S(1)}, u32[]{:S(2)}, u32[]{:S(2)}) %collective-permute-start.4) | collective-permute-done | bytes 131104 | tf_op jit(solution)/shard_map/ppermute | solution.py:304
  62.8 1.7 %collective-permute-start.7 = (bf16[256,256]{1,0:T(8,128)(2,1)S(1)}, bf16[256,256]{1,0:T(8,128)(2,1)S(1)}, u32[]{:S(2)}, u32[]{:S(2)}) collective-permute-start(bf16[256,256]{1,0:T(8,128)(2,1)S(1)} %collective-permute-done.4.refs_1_), channel_id=1, source_target_pairs={{0,128},{128,0},{1,129},{129,1},{2,130},{130,2},{3,131},{131,3},{4... | collective-permute-start | bytes 393224 | tf_op jit(solution)/shard_map/ppermute | solution.py:305
  64.5 0.0 collective-permute-done.2.refs_3_
  64.5 0.0 collective-permute-start.3
  64.5 0.0 collective-permute-done.6.refs_4_
  64.5 0.8 %early_products.1 = f32[256,1024]{1,0:T(8,128)S(1)} custom-call(bf16[256,256]{1,0:T(8,128)(2,1)S(1)} %pad_maximum_fusion.refs_0_, bf16[256,256]{1,0:T(8,128)(2,1)S(1)} %collective-permute-done.4.refs_1_, bf16[256,256]{1,0:T(8,128)(2,1)S(1)} %collective-permute-done.5.refs_2_, bf16[256,256]{1,0:T(8,128)(2,1)S(1)} %collective-permute-done.2.refs_3_, ...), custom_call_target="tpu_custom_call" | custom-call | flops 671088640 | bytes 4325376 | tf_op jit(solution)/shard_map/early_products/pallas_call | solution.py:173
  65.4 0.0 collective-permute-done.8
  65.4 0.3 fusion.2
  65.7 1.8 %collective-permute-done.7 = bf16[256,256]{1,0:T(8,128)(2,1)S(1)} collective-permute-done((bf16[256,256]{1,0:T(8,128)(2,1)S(1)}, bf16[256,256]{1,0:T(8,128)(2,1)S(1)}, u32[]{:S(2)}, u32[]{:S(2)}) %collective-permute-start.7) | collective-permute-done | bytes 131104 | tf_op jit(solution)/shard_map/ppermute | solution.py:305
  67.5 0.3 fusion.refs_1_
  67.8 2.3 %collective-permute-done.3.refs_0_ = bf16[256,256]{1,0:T(8,128)(2,1)S(1)} collective-permute-done((bf16[256,256]{1,0:T(8,128)(2,1)S(1)}, bf16[256,256]{1,0:T(8,128)(2,1)S(1)}, u32[]{:S(2)}, u32[]{:S(2)}) %collective-permute-start.3) | collective-permute-done | bytes 131104 | tf_op jit(solution)/shard_map/ppermute | solution.py:305
  70.1 0.3 late_products.1
  70.5 0.0 copy-start.2
  70.5 0.0 copy-start.3
  70.5 0.5 all-to-all-done.1
  71.0 1.6 %collective-permute-start.9 = (bf16[4,256,128]{2,1,0:T(8,128)(2,1)S(1)}, bf16[4,256,128]{2,1,0:T(8,128)(2,1)S(1)}, u32[]{:S(2)}, u32[]{:S(2)}) collective-permute-start(bf16[4,256,128]{2,1,0:T(8,128)(2,1)S(1)} %get-tuple-element.30), channel_id=1, source_target_pairs={{0,2},{2,0},{1,3},{3,1},{4,6},{6,4},{5,7},{7,5},{8,10},{10,8},{9,1... | collective-permute-start | bytes 786440 | tf_op jit(solution)/shard_map/ppermute | solution.py:314
  72.6 0.1 convert_element_type.32
  72.7 0.3 fusion.10
  73.0 0.1 copy.9
  73.1 0.1 multiply_reduce_fusion
  73.2 0.0 copy-done
  73.2 0.3 fusion.6
  73.5 0.0 copy-done.2
  73.5 0.0 copy-done.3
  73.5 0.1 bitcast_add_fusion
  73.6 0.1 collective-permute-done.9
  73.7 0.8 %fusion.5 = bf16[1024,128]{1,0:T(8,128)(2,1)} fusion(f32[1024,128]{1,0:T(8,128)S(1)} %bitcast_add_fusion, bf16[4,256,128]{2,1,0:T(8,128)(2,1)S(1)} %collective-permute-done.9), kind=kLoop, calls=%fused_computation.8 | loop fusion | flops 393216 | bytes 1048576 | tf_op jit(solution)/shard_map/convert_element_type | solution.py:323
  (7 shorter events, 0.0 us)
Async XLA Ops:
  0.0 73.2 %copy-start = (bf16[128,128]{1,0:T(8,128)(2,1)S(1)}, bf16[128,128]{1,0:T(8,128)(2,1)}, u32[]{:S(2)}) copy-start(bf16[128,128]{1,0:T(8,128)(2,1)} %param.13) | copy-start | bytes 98308
  0.0 58.2 %copy-start.1 = (bf16[1024,128]{1,0:T(8,128)(2,1)S(1)}, bf16[1024,128]{1,0:T(8,128)(2,1)}, u32[]{:S(2)}) copy-start(bf16[1024,128]{1,0:T(8,128)(2,1)} %weight_ref.5) | copy-start | bytes 786436
  3.1 36.1 %all-to-all-start = ((bf16[128,4,640]{2,1,0:T(4,128)(2,1)}), bf16[128,4,640]{2,1,0:T(4,128)(2,1)S(1)}, u32[]{:S(2)}, u32[]{:S(2)}) async-start(bf16[128,4,640]{2,1,0:T(4,128)(2,1)} %get-tuple-element.18), calls=%async_computation | async-start | bytes 1310720 | tf_op jit(solution)/shard_map/all_to_all | solution.py:292
  18.0 3.3 %collective-permute-start = (bf16[32,256]{1,0:T(8,128)(2,1)}, bf16[32,256]{1,0:T(8,128)(2,1)S(1)}, u32[]{:S(2)}, u32[]{:S(2)}) collective-permute-start(bf16[32,256]{1,0:T(8,128)(2,1)} %get-tuple-element.19), channel_id=1, source_target_pairs={{0,2},{2,0},{1,3},{3,1},{4,6},{6,4},{5,7},{7,5},{8,10},{10,8},{9,1... | collective-permute-start | bytes 49160 | tf_op jit(solution)/shard_map/ppermute | solution.py:291
  40.4 9.2 %collective-permute-start.1 = (bf16[384,128]{1,0:T(8,128)(2,1)S(1)}, bf16[384,128]{1,0:T(8,128)(2,1)S(1)}, u32[]{:S(2)}, u32[]{:S(2)}) collective-permute-start(bf16[384,128]{1,0:T(8,128)(2,1)S(1)} %get-tuple-element.25), channel_id=1, source_target_pairs={{0,1},{1,0},{2,3},{3,2},{4,5},{5,4},{6,7},{7,6},{8,9},{9,8},{10,11... | collective-permute-start | bytes 294920 | tf_op jit(solution)/shard_map/ppermute | solution.py:300
  42.8 28.1 %all-to-all-start.1 = ((bf16[256,4,256]{2,1,0:T(4,128)(2,1)}), bf16[256,4,256]{2,1,0:T(4,128)(2,1)S(1)}, u32[]{:S(2)}, u32[]{:S(2)}) async-start(bf16[256,4,256]{2,1,0:T(4,128)(2,1)} %get-tuple-element.27), calls=%async_computation.1 | async-start | bytes 1048576 | tf_op jit(solution)/shard_map/all_to_all | solution.py:298
  49.6 6.2 %collective-permute-start.5 = (bf16[256,256]{1,0:T(8,128)(2,1)S(1)}, bf16[256,256]{1,0:T(8,128)(2,1)S(1)}, u32[]{:S(2)}, u32[]{:S(2)}) collective-permute-start(bf16[256,256]{1,0:T(8,128)(2,1)S(1)} %pad_maximum_fusion.refs_0_), channel_id=1, source_target_pairs={{0,32},{32,64},{64,96},{96,0},{1,33},{33,65},{65,97},{97,1},{2,34}... | collective-permute-start | bytes 393224 | tf_op jit(solution)/shard_map/ppermute | solution.py:304
  51.1 11.7 %collective-permute-start.4 = (bf16[256,256]{1,0:T(8,128)(2,1)S(1)}, bf16[256,256]{1,0:T(8,128)(2,1)S(1)}, u32[]{:S(2)}, u32[]{:S(2)}) collective-permute-start(bf16[256,256]{1,0:T(8,128)(2,1)S(1)} %pad_maximum_fusion.refs_0_), channel_id=1, source_target_pairs={{0,64},{32,96},{64,0},{96,32},{1,65},{33,97},{65,1},{97,33},{2,66}... | collective-permute-start | bytes 393224 | tf_op jit(solution)/shard_map/ppermute | solution.py:304
  53.5 11.0 %collective-permute-start.2 = (bf16[256,256]{1,0:T(8,128)(2,1)S(1)}, bf16[256,256]{1,0:T(8,128)(2,1)S(1)}, u32[]{:S(2)}, u32[]{:S(2)}) collective-permute-start(bf16[256,256]{1,0:T(8,128)(2,1)S(1)} %pad_maximum_fusion.refs_0_), channel_id=1, source_target_pairs={{0,96},{32,0},{64,32},{96,64},{1,97},{33,1},{65,33},{97,65},{2,98}... | collective-permute-start | bytes 393224 | tf_op jit(solution)/shard_map/ppermute | solution.py:304
  54.6 9.9 %collective-permute-start.6 = (bf16[256,256]{1,0:T(8,128)(2,1)S(1)}, bf16[256,256]{1,0:T(8,128)(2,1)S(1)}, u32[]{:S(2)}, u32[]{:S(2)}) collective-permute-start(bf16[256,256]{1,0:T(8,128)(2,1)S(1)} %pad_maximum_fusion.refs_0_), channel_id=1, source_target_pairs={{0,128},{128,0},{1,129},{129,1},{2,130},{130,2},{3,131},{131,3},{4... | collective-permute-start | bytes 393224 | tf_op jit(solution)/shard_map/ppermute | solution.py:305
  55.8 9.6 %collective-permute-start.8 = (bf16[256,256]{1,0:T(8,128)(2,1)S(1)}, bf16[256,256]{1,0:T(8,128)(2,1)S(1)}, u32[]{:S(2)}, u32[]{:S(2)}) collective-permute-start(bf16[256,256]{1,0:T(8,128)(2,1)S(1)} %collective-permute-done.5.refs_2_), channel_id=1, source_target_pairs={{0,128},{128,0},{1,129},{129,1},{2,130},{130,2},{3,131},{131,3},{4... | collective-permute-start | bytes 393224 | tf_op jit(solution)/shard_map/ppermute | solution.py:305
  62.8 4.7 %collective-permute-start.7 = (bf16[256,256]{1,0:T(8,128)(2,1)S(1)}, bf16[256,256]{1,0:T(8,128)(2,1)S(1)}, u32[]{:S(2)}, u32[]{:S(2)}) collective-permute-start(bf16[256,256]{1,0:T(8,128)(2,1)S(1)} %collective-permute-done.4.refs_1_), channel_id=1, source_target_pairs={{0,128},{128,0},{1,129},{129,1},{2,130},{130,2},{3,131},{131,3},{4... | collective-permute-start | bytes 393224 | tf_op jit(solution)/shard_map/ppermute | solution.py:305
  64.5 5.6 %collective-permute-start.3 = (bf16[256,256]{1,0:T(8,128)(2,1)S(1)}, bf16[256,256]{1,0:T(8,128)(2,1)S(1)}, u32[]{:S(2)}, u32[]{:S(2)}) collective-permute-start(bf16[256,256]{1,0:T(8,128)(2,1)S(1)} %collective-permute-done.2.refs_3_), channel_id=1, source_target_pairs={{0,128},{128,0},{1,129},{129,1},{2,130},{130,2},{3,131},{131,3},{4... | collective-permute-start | bytes 393224 | tf_op jit(solution)/shard_map/ppermute | solution.py:305
  70.5 3.0 %copy-start.2 = (bf16[4,256,128]{2,1,0:T(8,128)(2,1)S(1)}, bf16[4,256,128]{2,1,0:T(8,128)(2,1)}, u32[]{:S(2)}) copy-start(bf16[4,256,128]{2,1,0:T(8,128)(2,1)} %state_ref.1) | copy-start | bytes 786436
  70.5 3.0 %copy-start.3 = (f32[1024,128]{1,0:T(8,128)S(1)}, f32[1024,128]{1,0:T(8,128)}, u32[]{:S(2)}) copy-start(f32[1024,128]{1,0:T(8,128)} %gates.1) | copy-start | bytes 1572868
  71.0 2.8 %collective-permute-start.9 = (bf16[4,256,128]{2,1,0:T(8,128)(2,1)S(1)}, bf16[4,256,128]{2,1,0:T(8,128)(2,1)S(1)}, u32[]{:S(2)}, u32[]{:S(2)}) collective-permute-start(bf16[4,256,128]{2,1,0:T(8,128)(2,1)S(1)} %get-tuple-element.30), channel_id=1, source_target_pairs={{0,2},{2,0},{1,3},{3,1},{4,6},{6,4},{5,7},{7,5},{8,10},{10,8},{9,1... | collective-permute-start | bytes 786440 | tf_op jit(solution)/shard_map/ppermute | solution.py:314

commit v5 on v4

--- a/solution.py
+++ b/solution.py
@@ -310,7 +310,6 @@
             turns[index], terms[index * depth : (index + 1) * depth], preferred_element_type=jnp.float32
         )
     opm, other = late_products(turns[7:], opm, terms, rows)
-    other, back = lax.optimization_barrier((other, back))
     other = lax.ppermute(other, "c", swap)
 
     back = back.reshape(nr, devs, points).astype(jnp.float32)

time: 74.8 us -> 74.8 us (level)
  transfers between devices with their start and end apart: 12 -> 12, of which waited for: 6 -> 5; matrix products, arithmetic and copies ran while one was open for 3% -> 3% of each run, Pallas kernels for 7% -> 7%
where the time goes in v5:
time: 74.8 us; the launch traced here: 74.5 us
  starting transfers between devices  37.4 us (50%)
  waiting for transfers between devices  24.1 us (32%)
  Pallas kernels  9.67 us (13%)
  other arithmetic  2.19 us (3%)
  matrix products  0.87 us (1%)
    all_to_all x1, waiting for transfers between devices, shards(): swapped = lax.all_to_all(send, DEV, split_axis=0, concat_axis=0, tiled=True)  17.2 us
    all_to_all x1, starting transfers between devices, shards(): swapped = lax.all_to_all(send, DEV, split_axis=0, concat_axis=0, tiled=True)  14.9 us
    all_to_all x1, starting transfers between devices, shards(): lax.all_to_all(partial, ('xh',) + DEV, split_axis=0, concat_axis=0, tiled...  6.7 us
    ppermute x4, starting transfers between devices, shards(): turns += [lax.ppermute(value, 'xl', swap) for value in turns]  5.23 us
    ppermute x3, starting transfers between devices, shards(): lax.ppermute(turns[0], 'y', [(i, (i + shift) % ny) for i in range(ny)])  5.05 us
    ppermute x4, waiting for transfers between devices, shards(): turns += [lax.ppermute(value, 'xl', swap) for value in turns]  4.15 us
    pallas_call x1, Pallas kernels, prepare(): pl.pallas_call(functools.partial(prepare_kernel, grid), out_shape=(jax.Sh...  3.11 us
    ppermute x3, waiting for transfers between devices, shards(): lax.ppermute(turns[0], 'y', [(i, (i + shift) % ny) for i in range(ny)])  2.64 us
  transfers between devices with their start and end apart: 12, of which 5 were waited for; matrix products, arithmetic and copies ran while one was open for 3% of the time, Pallas kernels for 7%

profile of v5, /device:TPU:1, one launch (start us, length us, event | category | flops | bytes accessed | tf_op | source)
XLA Modules:
  0.0 74.5 jit_solution(11332879340569639975)
XLA Ops:
  0.0 0.0 copy-start
  0.0 0.0 copy-start.1
  0.0 3.1 %prepare.1 = (bf16[128,4,640]{2,1,0:T(4,128)(2,1)}, bf16[32,256]{1,0:T(8,128)(2,1)}) custom-call(bf16[4,256,128]{2,1,0:T(8,128)(2,1)} %state_ref.1, s32[4,256]{1,0:T(4,128)} %mask_ref.1, bf16[64,4,64]{2,1,0:T(4,128)(2,1)} %align_ref.1, s32[4,64]{1,0:T(4,128)} %bitcast.27, bf16[128,640]{1,0:T(8,128)(2,1)} %weight_ref.4, bf16[64,64]{1,0:T(8,128)(2,1)} %align_weight_ref.1), custom_call_target="tpu_custom_call" | custom-call | tf_op jit(solution)/shard_map/prepare/pallas_call | solution.py:77
  3.1 14.9 %all-to-all-start = ((bf16[128,4,640]{2,1,0:T(4,128)(2,1)}), bf16[128,4,640]{2,1,0:T(4,128)(2,1)S(1)}, u32[]{:S(2)}, u32[]{:S(2)}) async-start(bf16[128,4,640]{2,1,0:T(4,128)(2,1)} %get-tuple-element.16), calls=%async_computation | async-start | bytes 1310720 | tf_op jit(solution)/shard_map/all_to_all | solution.py:292
  18.0 1.0 %collective-permute-start = (bf16[32,256]{1,0:T(8,128)(2,1)}, bf16[32,256]{1,0:T(8,128)(2,1)S(1)}, u32[]{:S(2)}, u32[]{:S(2)}) collective-permute-start(bf16[32,256]{1,0:T(8,128)(2,1)} %get-tuple-element.17), channel_id=1, source_target_pairs={{0,2},{2,0},{1,3},{3,1},{4,6},{6,4},{5,7},{7,5},{8,10},{10,8},{9,1... | collective-permute-start | bytes 49160 | tf_op jit(solution)/shard_map/ppermute | solution.py:291
  19.0 2.3 %gates.1 = f32[1024,128]{1,0:T(8,128)} custom-call(bf16[1024,128]{1,0:T(8,128)(2,1)} %bitcast.23, bf16[128,640]{1,0:T(8,128)(2,1)} %weight_ref.4), custom_call_target="tpu_custom_call" | custom-call | tf_op jit(solution)/shard_map/gates/pallas_call | solution.py:99
  21.3 0.0 collective-permute-done
  21.3 0.7 pad_maximum_fusion.1.first_ref
  22.0 17.2 %all-to-all-done.swapped_ref = bf16[128,4,640]{2,1,0:T(4,128)(2,1)S(1)} async-done(((bf16[128,4,640]{2,1,0:T(4,128)(2,1)}), bf16[128,4,640]{2,1,0:T(4,128)(2,1)S(1)}, u32[]{:S(2)}, u32[]{:S(2)}) %all-to-all-start) | async-done | bytes 655392 | tf_op jit(solution)/shard_map/all_to_all | solution.py:292
  39.2 1.2 %partials.1 = (bf16[256,4,256]{2,1,0:T(4,128)(2,1)}, bf16[256,128]{1,0:T(8,128)(2,1)S(1)}, bf16[384,128]{1,0:T(8,128)(2,1)S(1)}) custom-call(f32[8,128]{1,0:T(8,128)S(1)} %broadcast_in_dim.2.flag_ref, bf16[128,4,640]{2,1,0:T(4,128)(2,1)S(1)} %all-to-all-done.swapped_ref, bf16[32,512]{1,0:T(8,128)(2,1)S(1)} %pad_maximum_fusion.1.first_ref), custom_call_target="tpu_custom_call" | custom-call | tf_op jit(solution)/shard_map/partials/pallas_call | solution.py:257
  40.4 2.4 %collective-permute-start.1 = (bf16[384,128]{1,0:T(8,128)(2,1)S(1)}, bf16[384,128]{1,0:T(8,128)(2,1)S(1)}, u32[]{:S(2)}, u32[]{:S(2)}) collective-permute-start(bf16[384,128]{1,0:T(8,128)(2,1)S(1)} %get-tuple-element.24), channel_id=1, source_target_pairs={{0,1},{1,0},{2,3},{3,2},{4,5},{5,4},{6,7},{7,6},{8,9},{9,8},{10,11... | collective-permute-start | bytes 294920 | tf_op jit(solution)/shard_map/ppermute | solution.py:300
  42.8 6.7 %all-to-all-start.1 = ((bf16[256,4,256]{2,1,0:T(4,128)(2,1)}), bf16[256,4,256]{2,1,0:T(4,128)(2,1)S(1)}, u32[]{:S(2)}, u32[]{:S(2)}) async-start(bf16[256,4,256]{2,1,0:T(4,128)(2,1)} %get-tuple-element.22), calls=%async_computation.1 | async-start | bytes 1048576 | tf_op jit(solution)/shard_map/all_to_all | solution.py:298
  49.5 0.0 collective-permute-done.1
  49.6 1.5 %collective-permute-start.5 = (bf16[256,256]{1,0:T(8,128)(2,1)S(1)}, bf16[256,256]{1,0:T(8,128)(2,1)S(1)}, u32[]{:S(2)}, u32[]{:S(2)}) collective-permute-start(bf16[256,256]{1,0:T(8,128)(2,1)S(1)} %pad_maximum_fusion.refs_0_), channel_id=1, source_target_pairs={{0,32},{32,64},{64,96},{96,0},{1,33},{33,65},{65,97},{97,1},{2,34}... | collective-permute-start | bytes 393224 | tf_op jit(solution)/shard_map/ppermute | solution.py:304
  51.1 2.4 %collective-permute-start.4 = (bf16[256,256]{1,0:T(8,128)(2,1)S(1)}, bf16[256,256]{1,0:T(8,128)(2,1)S(1)}, u32[]{:S(2)}, u32[]{:S(2)}) collective-permute-start(bf16[256,256]{1,0:T(8,128)(2,1)S(1)} %pad_maximum_fusion.refs_0_), channel_id=1, source_target_pairs={{0,64},{32,96},{64,0},{96,32},{1,65},{33,97},{65,1},{97,33},{2,66}... | collective-permute-start | bytes 393224 | tf_op jit(solution)/shard_map/ppermute | solution.py:304
  53.5 1.1 %collective-permute-start.2 = (bf16[256,256]{1,0:T(8,128)(2,1)S(1)}, bf16[256,256]{1,0:T(8,128)(2,1)S(1)}, u32[]{:S(2)}, u32[]{:S(2)}) collective-permute-start(bf16[256,256]{1,0:T(8,128)(2,1)S(1)} %pad_maximum_fusion.refs_0_), channel_id=1, source_target_pairs={{0,96},{32,0},{64,32},{96,64},{1,97},{33,1},{65,33},{97,65},{2,98}... | collective-permute-start | bytes 393224 | tf_op jit(solution)/shard_map/ppermute | solution.py:304
  54.6 1.2 %collective-permute-start.6 = (bf16[256,256]{1,0:T(8,128)(2,1)S(1)}, bf16[256,256]{1,0:T(8,128)(2,1)S(1)}, u32[]{:S(2)}, u32[]{:S(2)}) collective-permute-start(bf16[256,256]{1,0:T(8,128)(2,1)S(1)} %pad_maximum_fusion.refs_0_), channel_id=1, source_target_pairs={{0,128},{128,0},{1,129},{129,1},{2,130},{130,2},{3,131},{131,3},{4... | collective-permute-start | bytes 393224 | tf_op jit(solution)/shard_map/ppermute | solution.py:305
  55.8 0.0 collective-permute-done.5.refs_2_
  55.8 2.3 %collective-permute-start.8 = (bf16[256,256]{1,0:T(8,128)(2,1)S(1)}, bf16[256,256]{1,0:T(8,128)(2,1)S(1)}, u32[]{:S(2)}, u32[]{:S(2)}) collective-permute-start(bf16[256,256]{1,0:T(8,128)(2,1)S(1)} %collective-permute-done.5.refs_2_), channel_id=1, source_target_pairs={{0,128},{128,0},{1,129},{129,1},{2,130},{130,2},{3,131},{131,3},{4... | collective-permute-start | bytes 393224 | tf_op jit(solution)/shard_map/ppermute | solution.py:305
  58.1 0.1 pad_add_fusion.place_ref
  58.2 0.0 copy-done.1
  58.2 1.9 %outer_terms.1.refs_5_.refs_2_ = bf16[2048,1024]{1,0:T(8,128)(2,1)S(1)} custom-call(s32[4]{0:T(128)S(1)} %pad_add_fusion.place_ref, bf16[32,512]{1,0:T(8,128)(2,1)S(1)} %pad_maximum_fusion.1.first_ref, bf16[128,128]{1,0:T(8,128)(2,1)S(1)} %slice.29.came_ref, bf16[1024,128]{1,0:T(8,128)(2,1)S(1)} %copy-done.1), custom_call_target="tpu_custom_call" | custom-call | flops 134217728 | bytes 4194304 | tf_op jit(solution)/shard_map/outer_terms/pallas_call | solution.py:146
  60.2 2.6 %collective-permute-done.4.refs_1_ = bf16[256,256]{1,0:T(8,128)(2,1)S(1)} collective-permute-done((bf16[256,256]{1,0:T(8,128)(2,1)S(1)}, bf16[256,256]{1,0:T(8,128)(2,1)S(1)}, u32[]{:S(2)}, u32[]{:S(2)}) %collective-permute-start.4) | collective-permute-done | bytes 131104 | tf_op jit(solution)/shard_map/ppermute | solution.py:304
  62.8 1.7 %collective-permute-start.7 = (bf16[256,256]{1,0:T(8,128)(2,1)S(1)}, bf16[256,256]{1,0:T(8,128)(2,1)S(1)}, u32[]{:S(2)}, u32[]{:S(2)}) collective-permute-start(bf16[256,256]{1,0:T(8,128)(2,1)S(1)} %collective-permute-done.4.refs_1_), channel_id=1, source_target_pairs={{0,128},{128,0},{1,129},{129,1},{2,130},{130,2},{3,131},{131,3},{4... | collective-permute-start | bytes 393224 | tf_op jit(solution)/shard_map/ppermute | solution.py:305
  64.5 0.0 collective-permute-done.2.refs_3_
  64.5 0.0 collective-permute-start.3
  64.5 0.0 collective-permute-done.6.refs_4_
  64.5 0.8 %early_products.1 = f32[256,1024]{1,0:T(8,128)S(1)} custom-call(bf16[256,256]{1,0:T(8,128)(2,1)S(1)} %pad_maximum_fusion.refs_0_, bf16[256,256]{1,0:T(8,128)(2,1)S(1)} %collective-permute-done.4.refs_1_, bf16[256,256]{1,0:T(8,128)(2,1)S(1)} %collective-permute-done.5.refs_2_, bf16[256,256]{1,0:T(8,128)(2,1)S(1)} %collective-permute-done.2.refs_3_, ...), custom_call_target="tpu_custom_call" | custom-call | flops 671088640 | bytes 4325376 | tf_op jit(solution)/shard_map/early_products/pallas_call | solution.py:173
  65.4 0.0 collective-permute-done.8
  65.4 0.3 fusion.1
  65.7 1.8 %collective-permute-done.7 = bf16[256,256]{1,0:T(8,128)(2,1)S(1)} collective-permute-done((bf16[256,256]{1,0:T(8,128)(2,1)S(1)}, bf16[256,256]{1,0:T(8,128)(2,1)S(1)}, u32[]{:S(2)}, u32[]{:S(2)}) %collective-permute-start.7) | collective-permute-done | bytes 131104 | tf_op jit(solution)/shard_map/ppermute | solution.py:305
  67.5 0.3 fusion.refs_1_
  67.8 2.3 %collective-permute-done.3.refs_0_ = bf16[256,256]{1,0:T(8,128)(2,1)S(1)} collective-permute-done((bf16[256,256]{1,0:T(8,128)(2,1)S(1)}, bf16[256,256]{1,0:T(8,128)(2,1)S(1)}, u32[]{:S(2)}, u32[]{:S(2)}) %collective-permute-start.3) | collective-permute-done | bytes 131104 | tf_op jit(solution)/shard_map/ppermute | solution.py:305
  70.1 0.3 late_products.1
  70.5 0.0 copy-start.2
  70.5 0.0 copy-start.3
  70.5 2.1 %collective-permute-start.9 = (bf16[4,256,128]{2,1,0:T(8,128)(2,1)S(1)}, bf16[4,256,128]{2,1,0:T(8,128)(2,1)S(1)}, u32[]{:S(2)}, u32[]{:S(2)}) collective-permute-start(bf16[4,256,128]{2,1,0:T(8,128)(2,1)S(1)} %get-tuple-element.26), channel_id=1, source_target_pairs={{0,2},{2,0},{1,3},{3,1},{4,6},{6,4},{5,7},{7,5},{8,10},{10,8},{9,1... | collective-permute-start | bytes 786440 | tf_op jit(solution)/shard_map/ppermute | solution.py:313
  72.6 0.0 all-to-all-done.1
  72.6 0.1 convert_element_type.32
  72.7 0.3 fusion.10
  73.0 0.1 copy.9
  73.1 0.1 multiply_reduce_fusion
  73.2 0.0 copy-done
  73.2 0.3 fusion.6
  73.5 0.0 copy-done.2
  73.5 0.0 copy-done.3
  73.5 0.1 bitcast_add_fusion
  73.6 0.1 collective-permute-done.9
  73.7 0.8 %fusion.5 = bf16[1024,128]{1,0:T(8,128)(2,1)} fusion(f32[1024,128]{1,0:T(8,128)S(1)} %bitcast_add_fusion, bf16[4,256,128]{2,1,0:T(8,128)(2,1)S(1)} %collective-permute-done.9), kind=kLoop, calls=%fused_computation.8 | loop fusion | flops 393216 | bytes 1048576 | tf_op jit(solution)/shard_map/convert_element_type | solution.py:322
  (7 shorter events, 0.0 us)
Async XLA Ops:
  0.0 73.2 %copy-start = (bf16[128,128]{1,0:T(8,128)(2,1)S(1)}, bf16[128,128]{1,0:T(8,128)(2,1)}, u32[]{:S(2)}) copy-start(bf16[128,128]{1,0:T(8,128)(2,1)} %param.13) | copy-start | bytes 98308
  0.0 58.2 %copy-start.1 = (bf16[1024,128]{1,0:T(8,128)(2,1)S(1)}, bf16[1024,128]{1,0:T(8,128)(2,1)}, u32[]{:S(2)}) copy-start(bf16[1024,128]{1,0:T(8,128)(2,1)} %weight_ref.5) | copy-start | bytes 786436
  3.1 36.1 %all-to-all-start = ((bf16[128,4,640]{2,1,0:T(4,128)(2,1)}), bf16[128,4,640]{2,1,0:T(4,128)(2,1)S(1)}, u32[]{:S(2)}, u32[]{:S(2)}) async-start(bf16[128,4,640]{2,1,0:T(4,128)(2,1)} %get-tuple-element.16), calls=%async_computation | async-start | bytes 1310720 | tf_op jit(solution)/shard_map/all_to_all | solution.py:292
  18.0 3.3 %collective-permute-start = (bf16[32,256]{1,0:T(8,128)(2,1)}, bf16[32,256]{1,0:T(8,128)(2,1)S(1)}, u32[]{:S(2)}, u32[]{:S(2)}) collective-permute-start(bf16[32,256]{1,0:T(8,128)(2,1)} %get-tuple-element.17), channel_id=1, source_target_pairs={{0,2},{2,0},{1,3},{3,1},{4,6},{6,4},{5,7},{7,5},{8,10},{10,8},{9,1... | collective-permute-start | bytes 49160 | tf_op jit(solution)/shard_map/ppermute | solution.py:291
  40.4 9.2 %collective-permute-start.1 = (bf16[384,128]{1,0:T(8,128)(2,1)S(1)}, bf16[384,128]{1,0:T(8,128)(2,1)S(1)}, u32[]{:S(2)}, u32[]{:S(2)}) collective-permute-start(bf16[384,128]{1,0:T(8,128)(2,1)S(1)} %get-tuple-element.24), channel_id=1, source_target_pairs={{0,1},{1,0},{2,3},{3,2},{4,5},{5,4},{6,7},{7,6},{8,9},{9,8},{10,11... | collective-permute-start | bytes 294920 | tf_op jit(solution)/shard_map/ppermute | solution.py:300
  42.8 29.7 %all-to-all-start.1 = ((bf16[256,4,256]{2,1,0:T(4,128)(2,1)}), bf16[256,4,256]{2,1,0:T(4,128)(2,1)S(1)}, u32[]{:S(2)}, u32[]{:S(2)}) async-start(bf16[256,4,256]{2,1,0:T(4,128)(2,1)} %get-tuple-element.22), calls=%async_computation.1 | async-start | bytes 1048576 | tf_op jit(solution)/shard_map/all_to_all | solution.py:298
  49.6 6.2 %collective-permute-start.5 = (bf16[256,256]{1,0:T(8,128)(2,1)S(1)}, bf16[256,256]{1,0:T(8,128)(2,1)S(1)}, u32[]{:S(2)}, u32[]{:S(2)}) collective-permute-start(bf16[256,256]{1,0:T(8,128)(2,1)S(1)} %pad_maximum_fusion.refs_0_), channel_id=1, source_target_pairs={{0,32},{32,64},{64,96},{96,0},{1,33},{33,65},{65,97},{97,1},{2,34}... | collective-permute-start | bytes 393224 | tf_op jit(solution)/shard_map/ppermute | solution.py:304
  51.1 11.7 %collective-permute-start.4 = (bf16[256,256]{1,0:T(8,128)(2,1)S(1)}, bf16[256,256]{1,0:T(8,128)(2,1)S(1)}, u32[]{:S(2)}, u32[]{:S(2)}) collective-permute-start(bf16[256,256]{1,0:T(8,128)(2,1)S(1)} %pad_maximum_fusion.refs_0_), channel_id=1, source_target_pairs={{0,64},{32,96},{64,0},{96,32},{1,65},{33,97},{65,1},{97,33},{2,66}... | collective-permute-start | bytes 393224 | tf_op jit(solution)/shard_map/ppermute | solution.py:304
  53.5 11.0 %collective-permute-start.2 = (bf16[256,256]{1,0:T(8,128)(2,1)S(1)}, bf16[256,256]{1,0:T(8,128)(2,1)S(1)}, u32[]{:S(2)}, u32[]{:S(2)}) collective-permute-start(bf16[256,256]{1,0:T(8,128)(2,1)S(1)} %pad_maximum_fusion.refs_0_), channel_id=1, source_target_pairs={{0,96},{32,0},{64,32},{96,64},{1,97},{33,1},{65,33},{97,65},{2,98}... | collective-permute-start | bytes 393224 | tf_op jit(solution)/shard_map/ppermute | solution.py:304
  54.6 9.9 %collective-permute-start.6 = (bf16[256,256]{1,0:T(8,128)(2,1)S(1)}, bf16[256,256]{1,0:T(8,128)(2,1)S(1)}, u32[]{:S(2)}, u32[]{:S(2)}) collective-permute-start(bf16[256,256]{1,0:T(8,128)(2,1)S(1)} %pad_maximum_fusion.refs_0_), channel_id=1, source_target_pairs={{0,128},{128,0},{1,129},{129,1},{2,130},{130,2},{3,131},{131,3},{4... | collective-permute-start | bytes 393224 | tf_op jit(solution)/shard_map/ppermute | solution.py:305
  55.8 9.6 %collective-permute-start.8 = (bf16[256,256]{1,0:T(8,128)(2,1)S(1)}, bf16[256,256]{1,0:T(8,128)(2,1)S(1)}, u32[]{:S(2)}, u32[]{:S(2)}) collective-permute-start(bf16[256,256]{1,0:T(8,128)(2,1)S(1)} %collective-permute-done.5.refs_2_), channel_id=1, source_target_pairs={{0,128},{128,0},{1,129},{129,1},{2,130},{130,2},{3,131},{131,3},{4... | collective-permute-start | bytes 393224 | tf_op jit(solution)/shard_map/ppermute | solution.py:305
  62.8 4.7 %collective-permute-start.7 = (bf16[256,256]{1,0:T(8,128)(2,1)S(1)}, bf16[256,256]{1,0:T(8,128)(2,1)S(1)}, u32[]{:S(2)}, u32[]{:S(2)}) collective-permute-start(bf16[256,256]{1,0:T(8,128)(2,1)S(1)} %collective-permute-done.4.refs_1_), channel_id=1, source_target_pairs={{0,128},{128,0},{1,129},{129,1},{2,130},{130,2},{3,131},{131,3},{4... | collective-permute-start | bytes 393224 | tf_op jit(solution)/shard_map/ppermute | solution.py:305
  64.5 5.6 %collective-permute-start.3 = (bf16[256,256]{1,0:T(8,128)(2,1)S(1)}, bf16[256,256]{1,0:T(8,128)(2,1)S(1)}, u32[]{:S(2)}, u32[]{:S(2)}) collective-permute-start(bf16[256,256]{1,0:T(8,128)(2,1)S(1)} %collective-permute-done.2.refs_3_), channel_id=1, source_target_pairs={{0,128},{128,0},{1,129},{129,1},{2,130},{130,2},{3,131},{131,3},{4... | collective-permute-start | bytes 393224 | tf_op jit(solution)/shard_map/ppermute | solution.py:305
  70.5 3.0 %copy-start.2 = (bf16[4,256,128]{2,1,0:T(8,128)(2,1)S(1)}, bf16[4,256,128]{2,1,0:T(8,128)(2,1)}, u32[]{:S(2)}) copy-start(bf16[4,256,128]{2,1,0:T(8,128)(2,1)} %state_ref.1) | copy-start | bytes 786436
  70.5 3.0 %copy-start.3 = (f32[1024,128]{1,0:T(8,128)S(1)}, f32[1024,128]{1,0:T(8,128)}, u32[]{:S(2)}) copy-start(f32[1024,128]{1,0:T(8,128)} %gates.1) | copy-start | bytes 1572868
  70.5 3.2 %collective-permute-start.9 = (bf16[4,256,128]{2,1,0:T(8,128)(2,1)S(1)}, bf16[4,256,128]{2,1,0:T(8,128)(2,1)S(1)}, u32[]{:S(2)}, u32[]{:S(2)}) collective-permute-start(bf16[4,256,128]{2,1,0:T(8,128)(2,1)S(1)} %get-tuple-element.26), channel_id=1, source_target_pairs={{0,2},{2,0},{1,3},{3,1},{4,6},{6,4},{5,7},{7,5},{8,10},{10,8},{9,1... | collective-permute-start | bytes 786440 | tf_op jit(solution)/shard_map/ppermute | solution.py:313
